TPU v7x, 256 devices: a whole 4x4x8 slice. The times are simulated.
256 devices in a mesh: redist: 32 (over z, x_lo, core), summa: 8 (over y, x_hi).
Axes of the slice: x: 4 (x_hi: 2, x_lo: 2; x = x_hi * 2 + x_lo), y: 4, z: 8, core: 2. Of those that a mesh axis runs over, the one named last changes fastest.
Arguments:
- amplitudes: float32 [1024, 22528], P('summa', 'redist'), may hold values from -6 to 6
- integrals: float32 [22528, 22528], P('redist', 'summa'), may hold values from -0.0390625 to 0.0390625
Outputs:
- ladder: float32 [1024, 22528], P('redist', 'summa')
All inputs are finite; a program needn't handle non-finite values.
Results may differ from a plain program's by a relative error of at most 0.000075.
Values sent between devices are 32-bit elements; how exact they have to be, the bound alone decides.
No kernel may reach another device: no remote copies, remote signals or barrier semaphores. Data moves between devices by JAX's collectives and lax.ppermute only.
A program may use at most 64 MiB of HBM per device.

v0:
```python
import functools

import jax
import jax.numpy as jnp
from jax import lax
from jax.experimental import pallas as pl
from jax.experimental.pallas import tpu as pltpu
from jax.sharding import Mesh, PartitionSpec as P

X_FIRST = 10
TILE = 256

SLOTS = 0x63745210

VMEM = pl.BlockSpec(memory_space=pltpu.VMEM)
SMEM = pl.BlockSpec(memory_space=pltpu.SMEM)
ANY = pl.BlockSpec(memory_space=pl.ANY)
HBM = pl.BlockSpec(memory_space=pltpu.HBM)

STEPS = ("zu", "zd", "x begin", "zu", "zd", "xu", "xd", "zu", "zd", "xu", "xd", "z end", "xu", "xd")

HEAVY, LIGHT = 20_000_000_000, 1


def shift(x, axis, by):
    n = lax.axis_size(axis)
    return lax.ppermute(x, axis, [(i, (i + by) % n) for i in range(n)])


def local(body, ins, deps, outs, scratch=(), scalars=(), through=(), pinned=True, big=(), weight=HEAVY, limit=4):
    pin = lambda x: pltpu.with_memory_space_constraint(x, pltpu.VMEM)
    sizes = [len(scalars), len(ins), len(big), len(through), len(deps), len(outs), len(through), len(scratch)]

    def kernel(*refs):
        groups, at = [], 0
        for n in sizes:
            groups.append(refs[at : at + n])
            at += n
        s, i, g, _, _, o, through_outs, t = groups
        body(*([s[0]] if s else []), [*i, *g], [*o, *through_outs], *([t] if t else []))

    kind = pltpu.VMEM if pinned else jax.ShapeDtypeStruct
    first = len(scalars) + len(ins) + len(big)
    return pl.pallas_call(
        kernel,
        in_specs=[SMEM] * len(scalars) + [VMEM] * len(ins) + [HBM] * len(big) + [VMEM] * len(through) + [ANY] * len(deps),
        out_specs=[VMEM] * (len(outs) + len(through)),
        out_shape=[kind(s, d) for s, d in outs] + [pltpu.VMEM(x.shape, x.dtype) for x in through],
        input_output_aliases={first + i: len(outs) + i for i in range(len(through))},
        scratch_shapes=list(scratch),
        compiler_params=pltpu.CompilerParams(vmem_limit_bytes=limit * 1024 * 1024),
        cost_estimate=pl.CostEstimate(flops=weight, bytes_accessed=1, transcendentals=0),
    )(*scalars, *map(pin, ins), *(pltpu.with_memory_space_constraint(x, pltpu.HBM) for x in big), *map(pin, through), *deps)


def split(x):
    high = x.astype(jnp.bfloat16)
    return high, (x - high.astype(jnp.float32)).astype(jnp.bfloat16)


def tile(i, first=0):
    return pl.ds(pl.multiple_of(first + i * TILE, 128), TILE)


def split_columns(b, sets, deps):
    depth, tiles = b.shape[0], b.shape[1] // TILE

    def body(ins, outs, scratch):
        held, sems = scratch

        def fetch(i):
            return pltpu.make_async_copy(ins[0].at[:, tile(i)], held.at[i], sems.at[i])

        for i in range(tiles):
            fetch(i).start()
        for j, (first, count) in enumerate(sets):

            @pl.loop(0, count)
            def _(i, j=j, first=first):
                fetch(first + i).wait()
                outs[2 * j][:, tile(i)], outs[2 * j + 1][:, tile(i)] = split(held[first + i])

    outs = [((depth, count * TILE), jnp.bfloat16) for _, count in sets for _ in range(2)]
    scratch = [pltpu.VMEM((tiles, depth, TILE), jnp.float32), pltpu.SemaphoreType.DMA((tiles,))]
    parts = local(body, [], deps, outs, scratch, big=[b], limit=12)
    return [parts[i : i + 2] for i in range(0, len(parts), 2)]


def products(panels, places, parts, deps, slots, into=(), joined=False, weight=HEAVY):
    count, depth = len(panels), parts[0][0].shape[0]
    mine = sorted({slot for *_, slot in places})
    first_slot, rows = mine[0], len(mine) * 64
    widths = [high.shape[1] for high, _ in parts]

    def body(ins, outs, scratch):
        a_high, a_low = scratch
        for ref, row, half, slot in places:
            to = half * rows + (slot - first_slot) * 64
            a_high[to : to + 64], a_low[to : to + 64] = split(ins[ref][row : row + 64])
        mul = functools.partial(jnp.dot, preferred_element_type=jnp.float32)
        block = slice(first_slot * 64, first_slot * 64 + rows)
        for j, width in enumerate(widths):
            high_ref, low_ref = ins[count + 2 * j : count + 2 * j + 2]
            keep_ref, send_ref = outs if joined else outs[2 * j : 2 * j + 2]
            first = sum(widths[:j]) if joined else 0
            for i in range(0, width, TILE):
                high, low = high_ref[:, i : i + TILE], low_ref[:, i : i + TILE]
                sums = mul(a_high[...], high) + (mul(a_low[...], high) + mul(a_high[...], low))
                keep_ref[block, first + i : first + i + TILE] = sums[:rows]
                send_ref[block, first + i : first + i + TILE] = sums[rows:]

    out_widths = [sum(widths)] if joined else widths
    outs = [] if into else [((slots * 64, width), jnp.float32) for width in out_widths for _ in range(2)]
    scratch = [pltpu.VMEM((2 * rows, depth), jnp.bfloat16)] * 2
    flat = [p for pair in parts for p in pair]
    return local(body, [*panels, *flat], deps, outs, scratch, through=into, weight=weight, limit=8)


def pack(up, down, other, deps):
    def body(ins, outs):
        up_ref, down_ref, other_ref = ins
        outs[0][:64], outs[0][64:] = other_ref[:64], up_ref[:64]
        outs[1][:64], outs[1][64:] = other_ref[64:], down_ref[64:]
        outs[2][:64], outs[2][64:] = up_ref[64:], down_ref[:64]

    return local(body, [up, down, other], deps, [(up.shape, jnp.float32)] * 3)


def late_halves(up, down, deps):
    def body(ins, outs):
        outs[0][...] = ins[0][:64]
        outs[1][...] = ins[1][:64]

    return local(body, [up, down], deps, [((64, up.shape[1]), jnp.float32)] * 2)


def x_part(lots, width, deps):
    def body(ins, outs):
        at = 0
        for kept, got, (_, _, col) in zip(ins[::2], ins[1::2], lots):
            for i in range(kept.shape[0] // 64):
                block = slice(64 * i + 32, 64 * i + 64), slice(col, col + width)
                outs[0][at : at + 32] = kept[block] + got[block]
                at += 32

    rows = sum(kept.shape[0] for kept, _, _ in lots) // 2
    return local(body, [v for lot in lots for v in lot[:2]], deps, [((rows, width), jnp.float32)], weight=LIGHT)[0]


def gate(deps):
    def body(ins, outs):
        outs[0][...] = jnp.zeros_like(outs[0])

    return local(body, [], deps, [((8, 128), jnp.float32)])


class Ring:
    def __init__(self, slots, lots, n, a, b, width):
        self.slots, self.lots, self.n, self.a, self.b, self.width = slots, lots, n, a, b, width

    def blocks(self, moves, outs, deps):
        n, width, arrays = self.n, self.width, []
        for _, lot in self.lots:
            arrays += [v for v, *_ in lot if not any(v is w for w in arrays)]
        where = lambda v: next(i for i, w in enumerate(arrays) if w is v)

        def body(slots, refs, out_refs):
            for out, at, k, low in moves:
                s = slots[k % 8]

                def write(first, lot):
                    starts = [pl.multiple_of((s - first) * stride + (row + low), n) for _, stride, row, _ in lot]

                    @pl.loop(0, width // TILE)
                    def _(i):
                        total = 0.0
                        for (v, _, _, col), start in zip(lot, starts):
                            total = total + refs[where(v)][pl.ds(start, n), tile(i, col)]
                        out_refs[out][at : at + n, tile(i)] = total

                for (first, end), lot in self.lots:
                    pl.when((s >= first) & (s < end))(functools.partial(write, first, lot))

        shapes = [((rows, width), jnp.float32) for rows in outs]
        return local(body, arrays, deps, shapes, scalars=[self.slots])

    def begin(self, deps):
        n, a, b = self.n, self.a, self.b
        moves = [(0, 0, 4, a), (0, n, 3, b), (1, 0, -4, b), (1, n, -3, a)]
        self.sends = list(self.blocks(moves, [2 * n, 2 * n], deps))
        return self.sends

    def hop(self, way):
        self.got[way].append(shift(self.sends[way], "z", 1 - 2 * way))

    def rest(self, deps):
        n, moves, rows = self.n, [], []
        for way, sign, long, short in ((0, 1, self.a, self.b), (1, -1, self.b, self.a)):
            for i in (3, 2, 1):
                moves.append((len(rows), 0, sign * i, long))
                if i > 1:
                    moves.append((len(rows), n, sign * (i - 1), short))
                rows.append(2 * n if i > 1 else n)
        moves += [(6, 0, 0, self.a), (7, 0, 0, self.b)]
        self.addends = self.blocks(moves, rows + [n, n], deps)
        self.got = [], []
        return self.addends[:1]

    def add(self, way, deps):
        got = self.got[way]
        addend = self.addends[3 * way + len(got) - 1]
        rows = addend.shape[0]

        def body(ins, outs):
            outs[0][...] = ins[0][:rows] + ins[1][...]

        self.sends[way] = local(body, [got[-1], addend], deps, [((rows, self.width), jnp.float32)])[0]
        return [self.sends[way]]

    def parts(self, which):
        return [self.addends[6 + which], self.got[which][3], self.got[1 - which][2]]


def add_up(terms, deps):
    n, width = terms[0].shape

    def body(ins, outs):
        outs[0][...] = ins[0][...] + ins[1][...] + ins[2][n:]

    return local(body, terms, deps, [((n, width), jnp.float32)])[0]


def finish(left, from_x, right_a, right_b):
    cut = from_x.shape[1]

    def body(ins, outs):
        total = lambda i: ins[i][...] + ins[i + 1][...] + ins[i + 2][ins[i].shape[0] :]
        outs[0][:, :cut] = 0.5 * (total(0) + ins[9][...])
        outs[0][:16, cut:] = 0.5 * total(3)
        outs[0][16:, cut:] = 0.5 * total(6)

    shape = (32, cut + right_a[0].shape[1])
    return local(body, [*left, *right_a, *right_b, from_x], [], [(shape, jnp.float32)], pinned=False)[0]


def per_device(amplitudes, integrals):
    z, xl, c = (lax.axis_index(n) for n in ("z", "xl", "c"))
    y, xh = lax.axis_index("y"), lax.axis_index("xh")
    depth, width = integrals.shape
    x_tiles = X_FIRST * 128 // TILE
    z_tiles = width // TILE - x_tiles

    owner = (z + jnp.arange(8, dtype=jnp.int32)) & 7
    code = (((owner >> 1) - y) & 3) * 2 + ((owner ^ xh) & 1)
    slots = (SLOTS >> (code * 4)) & 7

    own = amplitudes.reshape(2, 2, 32, depth)
    own = jnp.where(xl == 1, own[::-1], own)
    own = jnp.where(c == 1, own[:, ::-1], own)
    own = own.transpose(1, 0, 2, 3).reshape(128, depth)

    up, down, other = shift(own, "y", 1), shift(own, "y", -1), shift(own, "xh", 1)
    cut, x_width = z_tiles * TILE, x_tiles * TILE
    b_z, b_x = split_columns(integrals, ((0, z_tiles), (z_tiles, x_tiles)), [slots])
    both_halves = lambda ref, slot: [(ref, 64 * half, half, slot) for half in range(2)]
    own_blocks = products([own], both_halves(0, 0), [b_x, b_z], [], 4)
    packed_up, packed_down, packed_x = pack(up, down, other, [own_blocks[0]])
    up2, down2, other2 = shift(packed_up, "y", 1), shift(packed_down, "y", -1), shift(packed_x, "xh", 1)

    early_places = both_halves(0, 1) + both_halves(1, 2) + both_halves(2, 3)
    kept_x0, sent_x0, kept_z0, sent_z0 = products(
        [other, down, up], early_places, [b_x, b_z], [], 4, own_blocks, weight=LIGHT
    )
    got_x0, got_z0 = shift(sent_x0, "c", 1), shift(sent_z0, "c", 1)

    far_up, far_down = late_halves(up2, down2, [kept_z0, other2])
    other_far = [shift(far_up, "y", 1), shift(far_down, "y", -1)]
    x_send0 = x_part([(kept_x0, got_x0, 0)], x_width, [far_up])
    other0 = shift(x_send0, "xl", 1)

    late_places = [(0, 64, 0, 0), (1, 64, 1, 0), (2, 64, 0, 1), (1, 0, 1, 1), (0, 0, 0, 2), (2, 0, 1, 2)]
    kept1, sent1 = products([up2, down2, other2], late_places, [b_z, b_x], [x_send0], 3, joined=True)
    got1 = shift(sent1, "c", 1)
    kept_z2, sent_z2, kept_x2, sent_x2 = products(
        other_far, [(0, 0, 0, 0), (1, 0, 1, 0)], [b_z, b_x], [kept1, got_z0], 1
    )
    got_z2, got_x2 = shift(sent_z2, "c", 1), shift(sent_x2, "c", 1)

    z_lots = [
        ((0, 4), [(kept_z0, 64, 0, 0), (got_z0, 64, 0, 0)]),
        ((4, 7), [(kept1, 64, 0, 0), (got1, 64, 0, 0)]),
        ((7, 8), [(kept_z2, 64, 0, 0), (got_z2, 64, 0, 0)]),
    ]
    first = Ring(slots, z_lots, 32, 32, 0, cut)
    done = first.begin(gate([kept_z2]))
    done = first.rest(done)
    first.hop(0)
    first.hop(1)
    x_send1 = x_part([(kept1, got1, cut), (kept_x2, got_x2, 0)], x_width, [*done, other0])
    other1 = shift(x_send1, "xl", 1)
    x_lots = [
        ((0, 4), [(kept_x0, 64, 0, 0), (got_x0, 64, 0, 0), (other0, 32, 0, 0)]),
        ((4, 7), [(kept1, 64, 0, cut), (got1, 64, 0, cut), (other1, 32, 0, 0)]),
        ((7, 8), [(kept_x2, 64, 0, 0), (got_x2, 64, 0, 0), (other1, 32, 96, 0)]),
    ]
    second = Ring(slots, x_lots, 16, 0, 16, x_width)
    done = [x_send1]
    for step in STEPS:
        ring, way = (first, second)[step[0] == "x"], "ud".find(step[1])
        if step == "x begin":
            done = second.begin(done)
            done = second.rest(done)
            second.hop(0)
            second.hop(1)
        elif step == "z end":
            far_sum = add_up(first.parts(0), done)
            from_x = shift(far_sum, "xl", 1)
            done = [far_sum]
        else:
            done = ring.add(way, done)
            ring.hop(way)
    return finish(first.parts(1), from_x, second.parts(0), second.parts(1))


def solution(mesh):
    fine = Mesh(mesh.devices.reshape(8, 2, 2, 4, 2), ("z", "xl", "c", "y", "xh"))
    redist, summa = ("z", "xl", "c"), ("y", "xh")
    return jax.shard_map(
        per_device,
        mesh=fine,
        in_specs=(P(summa, redist), P(redist, summa)),
        out_specs=P(redist, summa),
        check_vma=False,
    )
```

profile of v0, /device:TPU:4, one launch (start us, length us, event | category | flops | bytes accessed | tf_op | source)
XLA Modules:
  0.0 108.4 jit_solution(7124452394024870129)
XLA Ops:
  1.3 1.7 %collective-permute-start.2 = (f32[128,704]{1,0:T(8,128)S(1)}, f32[128,704]{1,0:T(8,128)S(1)}, u32[]{:S(2)}, u32[]{:S(2)}) collective-permute-start(f32[128,704]{1,0:T(8,128)S(1)} %bitcast.4), channel_id=1, source_target_pairs={{0,2},{2,4},{4,6},{6,0},{1,3},{3,5},{5,7},{7,1},{8,10},{10,12},{12... | collective-permute-start | bytes 1081352 | tf_op jit(solution)/shard_map/ppermute | solution.py:27
  2.9 1.7 %collective-permute-start.1 = (f32[128,704]{1,0:T(8,128)S(1)}, f32[128,704]{1,0:T(8,128)S(1)}, u32[]{:S(2)}, u32[]{:S(2)}) collective-permute-start(f32[128,704]{1,0:T(8,128)S(1)} %bitcast.5), channel_id=1, source_target_pairs={{0,6},{2,0},{4,2},{6,4},{1,7},{3,1},{5,3},{7,5},{8,14},{10,8},{12,... | collective-permute-start | bytes 1081352 | tf_op jit(solution)/shard_map/ppermute | solution.py:27
  4.6 2.2 %collective-permute-start = (f32[128,704]{1,0:T(8,128)S(1)}, f32[128,704]{1,0:T(8,128)S(1)}, u32[]{:S(2)}, u32[]{:S(2)}) collective-permute-start(f32[128,704]{1,0:T(8,128)S(1)} %bitcast.6), channel_id=1, source_target_pairs={{0,1},{1,0},{2,3},{3,2},{4,5},{5,4},{6,7},{7,6},{8,9},{9,8},{10,11... | collective-permute-start | bytes 1081352 | tf_op jit(solution)/shard_map/ppermute | solution.py:27
  6.8 3.5 %shard_map.28 = (bf16[704,1536]{1,0:T(8,128)(2,1)S(1)}, bf16[704,1536]{1,0:T(8,128)(2,1)S(1)}, bf16[704,1280]{1,0:T(8,128)(2,1)S(1)}, bf16[704,1280]{1,0:T(8,128)(2,1)S(1)}) custom-call(f32[704,2816]{1,0:T(8,128)} %refs_0_.1, s32[8]{0:T(128)S(1)} %shift-right-arithmetic_and_fusion.refs_1_.refs_0_), custom_call_target="tpu_custom_call" | custom-call | flops 20000000000 | bytes 1 | tf_op jit(solution)/shard_map/pallas_call | solution.py:44
  10.4 1.9 %shard_map.29 = (f32[256,1280]{1,0:T(8,128)S(1)}, f32[256,1280]{1,0:T(8,128)S(1)}, f32[256,1536]{1,0:T(8,128)S(1)}, f32[256,1536]{1,0:T(8,128)S(1)}) custom-call(f32[128,704]{1,0:T(8,128)S(1)} %bitcast.7, bf16[704,1280]{1,0:T(8,128)(2,1)S(1)} %get-tuple-element.48.refs_1_.refs_3_.refs_5_.refs_4_, ...), custom_call_target="tpu_custom_call" | custom-call | flops 20000000000 | bytes 1 | tf_op jit(solution)/shard_map/pallas_call | solution.py:44
  12.2 1.2 %collective-permute-done.2.refs_2_.refs_0_ = f32[128,704]{1,0:T(8,128)S(1)} collective-permute-done((f32[128,704]{1,0:T(8,128)S(1)}, f32[128,704]{1,0:T(8,128)S(1)}, u32[]{:S(2)}, u32[]{:S(2)}) %collective-permute-start.2) | collective-permute-done | bytes 360480 | tf_op jit(solution)/shard_map/ppermute | solution.py:27
  13.5 3.0 %collective-permute-done.refs_0_.refs_2_ = f32[128,704]{1,0:T(8,128)S(1)} collective-permute-done((f32[128,704]{1,0:T(8,128)S(1)}, f32[128,704]{1,0:T(8,128)S(1)}, u32[]{:S(2)}, u32[]{:S(2)}) %collective-permute-start) | collective-permute-done | bytes 360480 | tf_op jit(solution)/shard_map/ppermute | solution.py:27
  16.9 3.0 %collective-permute-start.5 = (f32[128,704]{1,0:T(8,128)S(1)}, f32[128,704]{1,0:T(8,128)S(1)}, u32[]{:S(2)}, u32[]{:S(2)}) collective-permute-start(f32[128,704]{1,0:T(8,128)S(1)} %get-tuple-element.59), channel_id=1, source_target_pairs={{0,6},{2,0},{4,2},{6,4},{1,7},{3,1},{5,3},{7,5},{8,14},{10,8},{12,... | collective-permute-start | bytes 1081352 | tf_op jit(solution)/shard_map/ppermute | solution.py:27
  20.4 5.2 %shard_map.30 = (f32[256,1280]{1,0:T(8,128)S(1)}, f32[256,1280]{1,0:T(8,128)S(1)}, f32[256,1536]{1,0:T(8,128)S(1)}, f32[256,1536]{1,0:T(8,128)S(1)}) custom-call(f32[128,704]{1,0:T(8,128)S(1)} %collective-permute-done.refs_0_.refs_2_, ...), custom_call_target="tpu_custom_call", output_to_operand_aliasing={{0}: (7, {}), {1}: (8, {}), {2}: (9, {}), {3}: (10, {})} | custom-call | flops 1 | bytes 1 | tf_op jit(solution)/shard_map/pallas_call | solution.py:44
  27.4 3.0 %collective-permute-done.6.refs_3_.refs_2_ = f32[128,704]{1,0:T(8,128)S(1)} collective-permute-done((f32[128,704]{1,0:T(8,128)S(1)}, f32[128,704]{1,0:T(8,128)S(1)}, u32[]{:S(2)}, u32[]{:S(2)}) %collective-permute-start.6) | collective-permute-done | bytes 360480 | tf_op jit(solution)/shard_map/ppermute | solution.py:27
  30.8 1.7 %collective-permute-start.9 = (f32[64,704]{1,0:T(8,128)S(1)}, f32[64,704]{1,0:T(8,128)S(1)}, u32[]{:S(2)}, u32[]{:S(2)}) collective-permute-start(f32[64,704]{1,0:T(8,128)S(1)} %get-tuple-element.63.refs_2_), channel_id=1, source_target_pairs={{0,2},{2,4},{4,6},{6,0},{1,3},{3,5},{5,7},{7,1},{8,10},{10,12},{12... | collective-permute-start | bytes 540680 | tf_op jit(solution)/shard_map/ppermute | solution.py:27
  32.6 1.3 %collective-permute-start.15 = (f32[128,1280]{1,0:T(8,128)S(1)}, f32[128,1280]{1,0:T(8,128)S(1)}, u32[]{:S(2)}, u32[]{:S(2)}) collective-permute-start(f32[128,1280]{1,0:T(8,128)S(1)} %shard_map.33.refs_7_), channel_id=1, source_target_pairs={{0,16},{16,0},{1,17},{17,1},{2,18},{18,2},{3,19},{19,3},{4,20},{20... | collective-permute-start | bytes 1966088 | tf_op jit(solution)/shard_map/ppermute | solution.py:27
  33.9 5.2 %shard_map.34 = (f32[192,2816]{1,0:T(8,128)S(1)}, f32[192,2816]{1,0:T(8,128)S(1)}) custom-call(f32[128,704]{1,0:T(8,128)S(1)} %collective-permute-done.4.refs_0_, f32[128,704]{1,0:T(8,128)S(1)} %collective-permute-done.5.refs_1_, f32[128,704]{1,0:T(8,128)S(1)} %collective-permute-done.6.refs_3_.refs_2_, ...), custom_call_target="tpu_custom_call" | custom-call | flops 20000000000 | bytes 1 | tf_op jit(solution)/shard_map/pallas_call | solution.py:44
  39.2 1.9 %shard_map.35 = (f32[64,1536]{1,0:T(8,128)S(1)}, f32[64,1536]{1,0:T(8,128)S(1)}, f32[64,1280]{1,0:T(8,128)S(1)}, f32[64,1280]{1,0:T(8,128)S(1)}) custom-call(f32[64,704]{1,0:T(8,128)S(1)} %collective-permute-done.9.refs_0_, f32[64,704]{1,0:T(8,128)S(1)} %collective-permute-done.10.refs_1_, bf16[704,1536]{1,0:T(8,128)(2,1)S(1)} %get-tuple-element.50.refs_3_.refs_5_.refs_2_, ...), custom_call_target="tpu_custom_call" | custom-call | flops 20000000000 | bytes 1 | tf_op jit(solution)/shard_map/pallas_call | solution.py:44
  41.8 2.2 %collective-permute-done.11.refs_6_ = f32[64,1536]{1,0:T(8,128)S(1)} collective-permute-done((f32[64,1536]{1,0:T(8,128)S(1)}, f32[64,1536]{1,0:T(8,128)S(1)}, u32[]{:S(2)}, u32[]{:S(2)}) %collective-permute-start.11) | collective-permute-done | bytes 393248 | tf_op jit(solution)/shard_map/ppermute | solution.py:27
  44.9 2.0 %collective-permute-start.13 = (f32[64,1536]{1,0:T(8,128)S(1)}, f32[64,1536]{1,0:T(8,128)S(1)}, u32[]{:S(2)}, u32[]{:S(2)}) collective-permute-start(f32[64,1536]{1,0:T(8,128)S(1)} %get-tuple-element.69.refs_7_), channel_id=1, source_target_pairs={{0,32},{32,64},{64,96},{96,128},{128,160},{160,192},{192,224},{224... | collective-permute-start | bytes 1179656 | tf_op jit(solution)/shard_map/ppermute | solution.py:27
  46.8 4.0 %collective-permute-start.12 = (f32[64,1536]{1,0:T(8,128)S(1)}, f32[64,1536]{1,0:T(8,128)S(1)}, u32[]{:S(2)}, u32[]{:S(2)}) collective-permute-start(f32[64,1536]{1,0:T(8,128)S(1)} %get-tuple-element.70.refs_8_), channel_id=1, source_target_pairs={{0,224},{32,0},{64,32},{96,64},{128,96},{160,128},{192,160},{224,1... | collective-permute-start | bytes 1179656 | tf_op jit(solution)/shard_map/ppermute | solution.py:27
  50.9 1.4 %shard_map.38 = (f32[64,1536]{1,0:T(8,128)S(1)}, f32[64,1536]{1,0:T(8,128)S(1)}, f32[32,1536]{1,0:T(8,128)S(1)}, f32[64,1536]{1,0:T(8,128)S(1)}, f32[64,1536]{1,...) custom-call(s32[8]{0:T(128)S(1)} %shift-right-arithmetic_and_fusion.refs_1_.refs_0_, ...), custom_call_target="tpu_custom_call" | custom-call | flops 20000000000 | bytes 1 | tf_op jit(solution)/shard_map/pallas_call | solution.py:44
  53.3 6.9 %collective-permute-done.13.refs_0_ = f32[64,1536]{1,0:T(8,128)S(1)} collective-permute-done((f32[64,1536]{1,0:T(8,128)S(1)}, f32[64,1536]{1,0:T(8,128)S(1)}, u32[]{:S(2)}, u32[]{:S(2)}) %collective-permute-start.13) | collective-permute-done | bytes 393248 | tf_op jit(solution)/shard_map/ppermute | solution.py:27
  60.4 3.3 %collective-permute-start.16 = (f32[64,1536]{1,0:T(8,128)S(1)}, f32[64,1536]{1,0:T(8,128)S(1)}, u32[]{:S(2)}, u32[]{:S(2)}) collective-permute-start(f32[64,1536]{1,0:T(8,128)S(1)} %shard_map.41.refs_9_), channel_id=1, source_target_pairs={{0,224},{32,0},{64,32},{96,64},{128,96},{160,128},{192,160},{224,1... | collective-permute-start | bytes 1179656 | tf_op jit(solution)/shard_map/ppermute | solution.py:27
  63.7 5.3 %collective-permute-done.18.refs_6_ = f32[128,1280]{1,0:T(8,128)S(1)} collective-permute-done((f32[128,1280]{1,0:T(8,128)S(1)}, f32[128,1280]{1,0:T(8,128)S(1)}, u32[]{:S(2)}, u32[]{:S(2)}) %collective-permute-start.18) | collective-permute-done | bytes 655392 | tf_op jit(solution)/shard_map/ppermute | solution.py:27
  70.1 3.2 %collective-permute-start.21 = (f32[32,1280]{1,0:T(8,128)S(1)}, f32[32,1280]{1,0:T(8,128)S(1)}, u32[]{:S(2)}, u32[]{:S(2)}) collective-permute-start(f32[32,1280]{1,0:T(8,128)S(1)} %get-tuple-element.79.refs_10_), channel_id=1, source_target_pairs={{0,224},{32,0},{64,32},{96,64},{128,96},{160,128},{192,160},{224,1... | collective-permute-start | bytes 491528 | tf_op jit(solution)/shard_map/ppermute | solution.py:27
  73.3 1.4 %shard_map.43 = (f32[32,1280]{1,0:T(8,128)S(1)}, f32[32,1280]{1,0:T(8,128)S(1)}, f32[16,1280]{1,0:T(8,128)S(1)}, f32[32,1280]{1,0:T(8,128)S(1)}, f32[32,1280]{1,...) custom-call(s32[8]{0:T(128)S(1)} %shift-right-arithmetic_and_fusion.refs_1_.refs_0_, ...), custom_call_target="tpu_custom_call" | custom-call | flops 20000000000 | bytes 1 | tf_op jit(solution)/shard_map/pallas_call | solution.py:44
  74.9 3.3 %collective-permute-start.19 = (f32[64,1536]{1,0:T(8,128)S(1)}, f32[64,1536]{1,0:T(8,128)S(1)}, u32[]{:S(2)}, u32[]{:S(2)}) collective-permute-start(f32[64,1536]{1,0:T(8,128)S(1)} %shard_map.45.refs_2_), channel_id=1, source_target_pairs={{0,224},{32,0},{64,32},{96,64},{128,96},{160,128},{192,160},{224,1... | collective-permute-start | bytes 1179656 | tf_op jit(solution)/shard_map/ppermute | solution.py:27
  78.4 3.3 %collective-permute-start.27 = (f32[32,1280]{1,0:T(8,128)S(1)}, f32[32,1280]{1,0:T(8,128)S(1)}, u32[]{:S(2)}, u32[]{:S(2)}) collective-permute-start(f32[32,1280]{1,0:T(8,128)S(1)} %shard_map.47.refs_2_), channel_id=1, source_target_pairs={{0,224},{32,0},{64,32},{96,64},{128,96},{160,128},{192,160},{224,1... | collective-permute-start | bytes 491528 | tf_op jit(solution)/shard_map/ppermute | solution.py:27
  81.7 5.9 %collective-permute-done.20.refs_0_.refs_2_ = f32[64,1536]{1,0:T(8,128)S(1)} collective-permute-done((f32[64,1536]{1,0:T(8,128)S(1)}, f32[64,1536]{1,0:T(8,128)S(1)}, u32[]{:S(2)}, u32[]{:S(2)}) %collective-permute-start.20) | collective-permute-done | bytes 393248 | tf_op jit(solution)/shard_map/ppermute | solution.py:27
  87.7 3.3 %collective-permute-start.23 = (f32[32,1536]{1,0:T(8,128)S(1)}, f32[32,1536]{1,0:T(8,128)S(1)}, u32[]{:S(2)}, u32[]{:S(2)}) collective-permute-start(f32[32,1536]{1,0:T(8,128)S(1)} %shard_map.49.refs_2_), channel_id=1, source_target_pairs={{0,224},{32,0},{64,32},{96,64},{128,96},{160,128},{192,160},{224,1... | collective-permute-start | bytes 589832 | tf_op jit(solution)/shard_map/ppermute | solution.py:27
  91.2 3.3 %collective-permute-start.29 = (f32[32,1280]{1,0:T(8,128)S(1)}, f32[32,1280]{1,0:T(8,128)S(1)}, u32[]{:S(2)}, u32[]{:S(2)}) collective-permute-start(f32[32,1280]{1,0:T(8,128)S(1)} %shard_map.51.refs_3_), channel_id=1, source_target_pairs={{0,224},{32,0},{64,32},{96,64},{128,96},{160,128},{192,160},{224,1... | collective-permute-start | bytes 491528 | tf_op jit(solution)/shard_map/ppermute | solution.py:27
  95.9 1.7 %collective-permute-done.25.refs_0_.refs_8_ = f32[32,1280]{1,0:T(8,128)S(1)} collective-permute-done((f32[32,1280]{1,0:T(8,128)S(1)}, f32[32,1280]{1,0:T(8,128)S(1)}, u32[]{:S(2)}, u32[]{:S(2)}) %collective-permute-start.25) | collective-permute-done | bytes 163872 | tf_op jit(solution)/shard_map/ppermute | solution.py:27
  98.2 3.7 %collective-permute-start.30 = (f32[16,1280]{1,0:T(8,128)S(1)}, f32[16,1280]{1,0:T(8,128)S(1)}, u32[]{:S(2)}, u32[]{:S(2)}) collective-permute-start(f32[16,1280]{1,0:T(8,128)S(1)} %shard_map.54), channel_id=1, source_target_pairs={{0,224},{32,0},{64,32},{96,64},{128,96},{160,128},{192,160},{224,1... | collective-permute-start | bytes 245768 | tf_op jit(solution)/shard_map/ppermute | solution.py:27
  102.0 2.1 %collective-permute-done.30.refs_7_ = f32[16,1280]{1,0:T(8,128)S(1)} collective-permute-done((f32[16,1280]{1,0:T(8,128)S(1)}, f32[16,1280]{1,0:T(8,128)S(1)}, u32[]{:S(2)}, u32[]{:S(2)}) %collective-permute-start.30) | collective-permute-done | bytes 81952 | tf_op jit(solution)/shard_map/ppermute | solution.py:27
  104.0 3.6 %collective-permute-done.28.refs_4_ = f32[16,1280]{1,0:T(8,128)S(1)} collective-permute-done((f32[16,1280]{1,0:T(8,128)S(1)}, f32[16,1280]{1,0:T(8,128)S(1)}, u32[]{:S(2)}, u32[]{:S(2)}) %collective-permute-start.28) | collective-permute-done | bytes 81952 | tf_op jit(solution)/shard_map/ppermute | solution.py:27
  (65 shorter events, 11.8 us)
Async XLA Ops:
  1.3 12.2 %collective-permute-start.2 = (f32[128,704]{1,0:T(8,128)S(1)}, f32[128,704]{1,0:T(8,128)S(1)}, u32[]{:S(2)}, u32[]{:S(2)}) collective-permute-start(f32[128,704]{1,0:T(8,128)S(1)} %bitcast.4), channel_id=1, source_target_pairs={{0,2},{2,4},{4,6},{6,0},{1,3},{3,5},{5,7},{7,1},{8,10},{10,12},{12... | collective-permute-start | bytes 1081352 | tf_op jit(solution)/shard_map/ppermute | solution.py:27
  2.9 10.6 %collective-permute-start.1 = (f32[128,704]{1,0:T(8,128)S(1)}, f32[128,704]{1,0:T(8,128)S(1)}, u32[]{:S(2)}, u32[]{:S(2)}) collective-permute-start(f32[128,704]{1,0:T(8,128)S(1)} %bitcast.5), channel_id=1, source_target_pairs={{0,6},{2,0},{4,2},{6,4},{1,7},{3,1},{5,3},{7,5},{8,14},{10,8},{12,... | collective-permute-start | bytes 1081352 | tf_op jit(solution)/shard_map/ppermute | solution.py:27
  4.6 11.9 %collective-permute-start = (f32[128,704]{1,0:T(8,128)S(1)}, f32[128,704]{1,0:T(8,128)S(1)}, u32[]{:S(2)}, u32[]{:S(2)}) collective-permute-start(f32[128,704]{1,0:T(8,128)S(1)} %bitcast.6), channel_id=1, source_target_pairs={{0,1},{1,0},{2,3},{3,2},{4,5},{5,4},{6,7},{7,6},{8,9},{9,8},{10,11... | collective-permute-start | bytes 1081352 | tf_op jit(solution)/shard_map/ppermute | solution.py:27
  16.6 10.8 %collective-permute-start.4 = (f32[128,704]{1,0:T(8,128)S(1)}, f32[128,704]{1,0:T(8,128)S(1)}, u32[]{:S(2)}, u32[]{:S(2)}) collective-permute-start(f32[128,704]{1,0:T(8,128)S(1)} %get-tuple-element.58), channel_id=1, source_target_pairs={{0,2},{2,4},{4,6},{6,0},{1,3},{3,5},{5,7},{7,1},{8,10},{10,12},{12... | collective-permute-start | bytes 1081352 | tf_op jit(solution)/shard_map/ppermute | solution.py:27
  16.9 10.5 %collective-permute-start.5 = (f32[128,704]{1,0:T(8,128)S(1)}, f32[128,704]{1,0:T(8,128)S(1)}, u32[]{:S(2)}, u32[]{:S(2)}) collective-permute-start(f32[128,704]{1,0:T(8,128)S(1)} %get-tuple-element.59), channel_id=1, source_target_pairs={{0,6},{2,0},{4,2},{6,4},{1,7},{3,1},{5,3},{7,5},{8,14},{10,8},{12,... | collective-permute-start | bytes 1081352 | tf_op jit(solution)/shard_map/ppermute | solution.py:27
  19.9 10.5 %collective-permute-start.6 = (f32[128,704]{1,0:T(8,128)S(1)}, f32[128,704]{1,0:T(8,128)S(1)}, u32[]{:S(2)}, u32[]{:S(2)}) collective-permute-start(f32[128,704]{1,0:T(8,128)S(1)} %get-tuple-element.60), channel_id=1, source_target_pairs={{0,1},{1,0},{2,3},{3,2},{4,5},{5,4},{6,7},{7,6},{8,9},{9,8},{10,11... | collective-permute-start | bytes 1081352 | tf_op jit(solution)/shard_map/ppermute | solution.py:27
  25.6 6.9 %collective-permute-start.7 = (f32[256,1280]{1,0:T(8,128)S(1)}, f32[256,1280]{1,0:T(8,128)S(1)}, u32[]{:S(2)}, u32[]{:S(2)}) collective-permute-start(f32[256,1280]{1,0:T(8,128)S(1)} %get-tuple-element.62), channel_id=1, source_target_pairs={{0,8},{8,0},{1,9},{9,1},{2,10},{10,2},{3,11},{11,3},{4,12},{12,4},... | collective-permute-start | bytes 3932168 | tf_op jit(solution)/shard_map/ppermute | solution.py:27
  25.7 13.5 %collective-permute-start.3 = (f32[256,1536]{1,0:T(8,128)S(1)}, f32[256,1536]{1,0:T(8,128)S(1)}, u32[]{:S(2)}, u32[]{:S(2)}) collective-permute-start(f32[256,1536]{1,0:T(8,128)S(1)} %get-tuple-element.57), channel_id=1, source_target_pairs={{0,8},{8,0},{1,9},{9,1},{2,10},{10,2},{3,11},{11,3},{4,12},{12,4},... | collective-permute-start | bytes 4718600 | tf_op jit(solution)/shard_map/ppermute | solution.py:27
  30.4 8.8 %collective-permute-start.10 = (f32[64,704]{1,0:T(8,128)S(1)}, f32[64,704]{1,0:T(8,128)S(1)}, u32[]{:S(2)}, u32[]{:S(2)}) collective-permute-start(f32[64,704]{1,0:T(8,128)S(1)} %get-tuple-element.66), channel_id=1, source_target_pairs={{0,6},{2,0},{4,2},{6,4},{1,7},{3,1},{5,3},{7,5},{8,14},{10,8},{12,... | collective-permute-start | bytes 540680 | tf_op jit(solution)/shard_map/ppermute | solution.py:27
  30.8 8.4 %collective-permute-start.9 = (f32[64,704]{1,0:T(8,128)S(1)}, f32[64,704]{1,0:T(8,128)S(1)}, u32[]{:S(2)}, u32[]{:S(2)}) collective-permute-start(f32[64,704]{1,0:T(8,128)S(1)} %get-tuple-element.63.refs_2_), channel_id=1, source_target_pairs={{0,2},{2,4},{4,6},{6,0},{1,3},{3,5},{5,7},{7,1},{8,10},{10,12},{12... | collective-permute-start | bytes 540680 | tf_op jit(solution)/shard_map/ppermute | solution.py:27
  32.6 19.7 %collective-permute-start.15 = (f32[128,1280]{1,0:T(8,128)S(1)}, f32[128,1280]{1,0:T(8,128)S(1)}, u32[]{:S(2)}, u32[]{:S(2)}) collective-permute-start(f32[128,1280]{1,0:T(8,128)S(1)} %shard_map.33.refs_7_), channel_id=1, source_target_pairs={{0,16},{16,0},{1,17},{17,1},{2,18},{18,2},{3,19},{19,3},{4,20},{20... | collective-permute-start | bytes 1966088 | tf_op jit(solution)/shard_map/ppermute | solution.py:27
  39.1 4.9 %collective-permute-start.8 = (f32[192,2816]{1,0:T(8,128)S(1)}, f32[192,2816]{1,0:T(8,128)S(1)}, u32[]{:S(2)}, u32[]{:S(2)}) collective-permute-start(f32[192,2816]{1,0:T(8,128)S(1)} %get-tuple-element.65), channel_id=1, source_target_pairs={{0,8},{8,0},{1,9},{9,1},{2,10},{10,2},{3,11},{11,3},{4,12},{12,4},... | collective-permute-start | bytes 6488072 | tf_op jit(solution)/shard_map/ppermute | solution.py:27
  41.1 2.9 %collective-permute-start.11 = (f32[64,1536]{1,0:T(8,128)S(1)}, f32[64,1536]{1,0:T(8,128)S(1)}, u32[]{:S(2)}, u32[]{:S(2)}) collective-permute-start(f32[64,1536]{1,0:T(8,128)S(1)} %get-tuple-element.68), channel_id=1, source_target_pairs={{0,8},{8,0},{1,9},{9,1},{2,10},{10,2},{3,11},{11,3},{4,12},{12,4},... | collective-permute-start | bytes 1179656 | tf_op jit(solution)/shard_map/ppermute | solution.py:27
  41.7 10.6 %collective-permute-start.14 = (f32[64,1280]{1,0:T(8,128)S(1)}, f32[64,1280]{1,0:T(8,128)S(1)}, u32[]{:S(2)}, u32[]{:S(2)}) collective-permute-start(f32[64,1280]{1,0:T(8,128)S(1)} %get-tuple-element.75), channel_id=1, source_target_pairs={{0,8},{8,0},{1,9},{9,1},{2,10},{10,2},{3,11},{11,3},{4,12},{12,4},... | collective-permute-start | bytes 983048 | tf_op jit(solution)/shard_map/ppermute | solution.py:27
  44.9 15.3 %collective-permute-start.13 = (f32[64,1536]{1,0:T(8,128)S(1)}, f32[64,1536]{1,0:T(8,128)S(1)}, u32[]{:S(2)}, u32[]{:S(2)}) collective-permute-start(f32[64,1536]{1,0:T(8,128)S(1)} %get-tuple-element.69.refs_7_), channel_id=1, source_target_pairs={{0,32},{32,64},{64,96},{96,128},{128,160},{160,192},{192,224},{224... | collective-permute-start | bytes 1179656 | tf_op jit(solution)/shard_map/ppermute | solution.py:27
  46.8 13.5 %collective-permute-start.12 = (f32[64,1536]{1,0:T(8,128)S(1)}, f32[64,1536]{1,0:T(8,128)S(1)}, u32[]{:S(2)}, u32[]{:S(2)}) collective-permute-start(f32[64,1536]{1,0:T(8,128)S(1)} %get-tuple-element.70.refs_8_), channel_id=1, source_target_pairs={{0,224},{32,0},{64,32},{96,64},{128,96},{160,128},{192,160},{224,1... | collective-permute-start | bytes 1179656 | tf_op jit(solution)/shard_map/ppermute | solution.py:27
  52.4 16.6 %collective-permute-start.18 = (f32[128,1280]{1,0:T(8,128)S(1)}, f32[128,1280]{1,0:T(8,128)S(1)}, u32[]{:S(2)}, u32[]{:S(2)}) collective-permute-start(f32[128,1280]{1,0:T(8,128)S(1)} %shard_map.39.refs_2_), channel_id=1, source_target_pairs={{0,16},{16,0},{1,17},{17,1},{2,18},{18,2},{3,19},{19,3},{4,20},{20... | collective-permute-start | bytes 1966088 | tf_op jit(solution)/shard_map/ppermute | solution.py:27
  60.3 14.5 %collective-permute-start.17 = (f32[64,1536]{1,0:T(8,128)S(1)}, f32[64,1536]{1,0:T(8,128)S(1)}, u32[]{:S(2)}, u32[]{:S(2)}) collective-permute-start(f32[64,1536]{1,0:T(8,128)S(1)} %shard_map.40.refs_2_), channel_id=1, source_target_pairs={{0,32},{32,64},{64,96},{96,128},{128,160},{160,192},{192,224},{224... | collective-permute-start | bytes 1179656 | tf_op jit(solution)/shard_map/ppermute | solution.py:27
  60.4 14.4 %collective-permute-start.16 = (f32[64,1536]{1,0:T(8,128)S(1)}, f32[64,1536]{1,0:T(8,128)S(1)}, u32[]{:S(2)}, u32[]{:S(2)}) collective-permute-start(f32[64,1536]{1,0:T(8,128)S(1)} %shard_map.41.refs_9_), channel_id=1, source_target_pairs={{0,224},{32,0},{64,32},{96,64},{128,96},{160,128},{192,160},{224,1... | collective-permute-start | bytes 1179656 | tf_op jit(solution)/shard_map/ppermute | solution.py:27
  70.0 8.2 %collective-permute-start.22 = (f32[32,1280]{1,0:T(8,128)S(1)}, f32[32,1280]{1,0:T(8,128)S(1)}, u32[]{:S(2)}, u32[]{:S(2)}) collective-permute-start(f32[32,1280]{1,0:T(8,128)S(1)} %get-tuple-element.78.refs_9_), channel_id=1, source_target_pairs={{0,32},{32,64},{64,96},{96,128},{128,160},{160,192},{192,224},{224... | collective-permute-start | bytes 491528 | tf_op jit(solution)/shard_map/ppermute | solution.py:27
  70.1 8.2 %collective-permute-start.21 = (f32[32,1280]{1,0:T(8,128)S(1)}, f32[32,1280]{1,0:T(8,128)S(1)}, u32[]{:S(2)}, u32[]{:S(2)}) collective-permute-start(f32[32,1280]{1,0:T(8,128)S(1)} %get-tuple-element.79.refs_10_), channel_id=1, source_target_pairs={{0,224},{32,0},{64,32},{96,64},{128,96},{160,128},{192,160},{224,1... | collective-permute-start | bytes 491528 | tf_op jit(solution)/shard_map/ppermute | solution.py:27
  74.8 12.8 %collective-permute-start.20 = (f32[64,1536]{1,0:T(8,128)S(1)}, f32[64,1536]{1,0:T(8,128)S(1)}, u32[]{:S(2)}, u32[]{:S(2)}) collective-permute-start(f32[64,1536]{1,0:T(8,128)S(1)} %shard_map.44.refs_2_), channel_id=1, source_target_pairs={{0,32},{32,64},{64,96},{96,128},{128,160},{160,192},{192,224},{224... | collective-permute-start | bytes 1179656 | tf_op jit(solution)/shard_map/ppermute | solution.py:27
  74.9 12.7 %collective-permute-start.19 = (f32[64,1536]{1,0:T(8,128)S(1)}, f32[64,1536]{1,0:T(8,128)S(1)}, u32[]{:S(2)}, u32[]{:S(2)}) collective-permute-start(f32[64,1536]{1,0:T(8,128)S(1)} %shard_map.45.refs_2_), channel_id=1, source_target_pairs={{0,224},{32,0},{64,32},{96,64},{128,96},{160,128},{192,160},{224,1... | collective-permute-start | bytes 1179656 | tf_op jit(solution)/shard_map/ppermute | solution.py:27
  78.2 12.8 %collective-permute-start.24 = (f32[32,1280]{1,0:T(8,128)S(1)}, f32[32,1280]{1,0:T(8,128)S(1)}, u32[]{:S(2)}, u32[]{:S(2)}) collective-permute-start(f32[32,1280]{1,0:T(8,128)S(1)} %shard_map.46.refs_2_), channel_id=1, source_target_pairs={{0,32},{32,64},{64,96},{96,128},{128,160},{160,192},{192,224},{224... | collective-permute-start | bytes 491528 | tf_op jit(solution)/shard_map/ppermute | solution.py:27
  78.4 12.8 %collective-permute-start.27 = (f32[32,1280]{1,0:T(8,128)S(1)}, f32[32,1280]{1,0:T(8,128)S(1)}, u32[]{:S(2)}, u32[]{:S(2)}) collective-permute-start(f32[32,1280]{1,0:T(8,128)S(1)} %shard_map.47.refs_2_), channel_id=1, source_target_pairs={{0,224},{32,0},{64,32},{96,64},{128,96},{160,128},{192,160},{224,1... | collective-permute-start | bytes 491528 | tf_op jit(solution)/shard_map/ppermute | solution.py:27
  87.6 7.4 %collective-permute-start.26 = (f32[32,1536]{1,0:T(8,128)S(1)}, f32[32,1536]{1,0:T(8,128)S(1)}, u32[]{:S(2)}, u32[]{:S(2)}) collective-permute-start(f32[32,1536]{1,0:T(8,128)S(1)} %shard_map.48.refs_2_), channel_id=1, source_target_pairs={{0,32},{32,64},{64,96},{96,128},{128,160},{160,192},{192,224},{224... | collective-permute-start | bytes 589832 | tf_op jit(solution)/shard_map/ppermute | solution.py:27
  87.7 14.3 %collective-permute-start.23 = (f32[32,1536]{1,0:T(8,128)S(1)}, f32[32,1536]{1,0:T(8,128)S(1)}, u32[]{:S(2)}, u32[]{:S(2)}) collective-permute-start(f32[32,1536]{1,0:T(8,128)S(1)} %shard_map.49.refs_2_), channel_id=1, source_target_pairs={{0,224},{32,0},{64,32},{96,64},{128,96},{160,128},{192,160},{224,1... | collective-permute-start | bytes 589832 | tf_op jit(solution)/shard_map/ppermute | solution.py:27
  91.1 6.6 %collective-permute-start.25 = (f32[32,1280]{1,0:T(8,128)S(1)}, f32[32,1280]{1,0:T(8,128)S(1)}, u32[]{:S(2)}, u32[]{:S(2)}) collective-permute-start(f32[32,1280]{1,0:T(8,128)S(1)} %shard_map.50.refs_2_), channel_id=1, source_target_pairs={{0,32},{32,64},{64,96},{96,128},{128,160},{160,192},{192,224},{224... | collective-permute-start | bytes 491528 | tf_op jit(solution)/shard_map/ppermute | solution.py:27
  91.2 7.0 %collective-permute-start.29 = (f32[32,1280]{1,0:T(8,128)S(1)}, f32[32,1280]{1,0:T(8,128)S(1)}, u32[]{:S(2)}, u32[]{:S(2)}) collective-permute-start(f32[32,1280]{1,0:T(8,128)S(1)} %shard_map.51.refs_3_), channel_id=1, source_target_pairs={{0,224},{32,0},{64,32},{96,64},{128,96},{160,128},{192,160},{224,1... | collective-permute-start | bytes 491528 | tf_op jit(solution)/shard_map/ppermute | solution.py:27
  95.0 12.6 %collective-permute-start.31 = (f32[32,1536]{1,0:T(8,128)S(1)}, f32[32,1536]{1,0:T(8,128)S(1)}, u32[]{:S(2)}, u32[]{:S(2)}) collective-permute-start(f32[32,1536]{1,0:T(8,128)S(1)} %shard_map.52.refs_2_), channel_id=1, source_target_pairs={{0,16},{16,0},{1,17},{17,1},{2,18},{18,2},{3,19},{19,3},{4,20},{20... | collective-permute-start | bytes 589832 | tf_op jit(solution)/shard_map/ppermute | solution.py:27
  98.2 5.8 %collective-permute-start.30 = (f32[16,1280]{1,0:T(8,128)S(1)}, f32[16,1280]{1,0:T(8,128)S(1)}, u32[]{:S(2)}, u32[]{:S(2)}) collective-permute-start(f32[16,1280]{1,0:T(8,128)S(1)} %shard_map.54), channel_id=1, source_target_pairs={{0,224},{32,0},{64,32},{96,64},{128,96},{160,128},{192,160},{224,1... | collective-permute-start | bytes 245768 | tf_op jit(solution)/shard_map/ppermute | solution.py:27
  102.0 5.7 %collective-permute-start.28 = (f32[16,1280]{1,0:T(8,128)S(1)}, f32[16,1280]{1,0:T(8,128)S(1)}, u32[]{:S(2)}, u32[]{:S(2)}) collective-permute-start(f32[16,1280]{1,0:T(8,128)S(1)} %shard_map.53.refs_2_), channel_id=1, source_target_pairs={{0,32},{32,64},{64,96},{96,128},{128,160},{160,192},{192,224},{224... | collective-permute-start | bytes 245768 | tf_op jit(solution)/shard_map/ppermute | solution.py:27
where the time goes:
time: 109 us; the launch traced here: 108 us
  starting transfers between devices  45.9 us (42%)
  waiting for transfers between devices  37.2 us (34%)
  Pallas kernels  23.8 us (22%)
  local copies, waits for them, and re-layouts  1.17 us (1%)
    ppermute x32, starting transfers between devices, shift(): return lax.ppermute(x, axis, [(i, (i + by) % n) for i in range(n)])  45.9 us
    ppermute x32, waiting for transfers between devices, shift(): return lax.ppermute(x, axis, [(i, (i + by) % n) for i in range(n)])  37.2 us
    pallas_call x28, Pallas kernels, local(): pl.pallas_call(kernel, in_specs=[SMEM] * len(scalars) + [VMEM] * len(ins)...  23.8 us
  transfers between devices with their start and end apart: 32, of which 14 were waited for; matrix products, arithmetic and copies ran while one was open for 0% of the time, Pallas kernels for 21%

commit v1 on v0

--- a/solution.py
+++ b/solution.py
@@ -17,7 +17,7 @@
 ANY = pl.BlockSpec(memory_space=pl.ANY)
 HBM = pl.BlockSpec(memory_space=pltpu.HBM)
 
-STEPS = ("zu", "zd", "x begin", "zu", "zd", "xu", "xd", "zu", "zd", "xu", "xd", "z end", "xu", "xd")
+STEPS = ("zu", "zd", "x begin", "zu", "zd", "x rest", "xu", "xd", "zu", "zd", "xu", "xd", "z end", "xu", "xd")
 
 HEAVY, LIGHT = 20_000_000_000, 1
 
@@ -131,7 +131,7 @@
         outs[0][...] = ins[0][:64]
         outs[1][...] = ins[1][:64]
 
-    return local(body, [up, down], deps, [((64, up.shape[1]), jnp.float32)] * 2)
+    return local(body, [up, down], deps, [((64, up.shape[1]), jnp.float32)] * 2, weight=LIGHT)
 
 
 def x_part(lots, width, deps):
@@ -188,10 +188,12 @@
         n, a, b = self.n, self.a, self.b
         moves = [(0, 0, 4, a), (0, n, 3, b), (1, 0, -4, b), (1, n, -3, a)]
         self.sends = list(self.blocks(moves, [2 * n, 2 * n], deps))
+        self.got = [], []
         return self.sends
 
     def hop(self, way):
-        self.got[way].append(shift(self.sends[way], "z", 1 - 2 * way))
+        pairs = [(2 * z + c, 2 * ((z + (1 - 2 * way) * (1 - 2 * c)) % 8) + c) for z in range(8) for c in range(2)]
+        self.got[way].append(lax.ppermute(self.sends[way], ("z", "c"), pairs))
 
     def rest(self, deps):
         n, moves, rows = self.n, [], []
@@ -203,7 +205,6 @@
                 rows.append(2 * n if i > 1 else n)
         moves += [(6, 0, 0, self.a), (7, 0, 0, self.b)]
         self.addends = self.blocks(moves, rows + [n, n], deps)
-        self.got = [], []
         return self.addends[:1]
 
     def add(self, way, deps):
@@ -250,7 +251,7 @@
     x_tiles = X_FIRST * 128 // TILE
     z_tiles = width // TILE - x_tiles
 
-    owner = (z + jnp.arange(8, dtype=jnp.int32)) & 7
+    owner = (z + (1 - 2 * c) * jnp.arange(8, dtype=jnp.int32)) & 7
     code = (((owner >> 1) - y) & 3) * 2 + ((owner ^ xh) & 1)
     slots = (SLOTS >> (code * 4)) & 7
 
@@ -273,13 +274,13 @@
     )
     got_x0, got_z0 = shift(sent_x0, "c", 1), shift(sent_z0, "c", 1)
 
-    far_up, far_down = late_halves(up2, down2, [kept_z0, other2])
+    x_send0 = x_part([(kept_x0, got_x0, 0)], x_width, gate([kept_z0, up2, down2, other2]))
+    other0 = shift(x_send0, "xl", 1)
+    far_up, far_down = late_halves(up2, down2, [x_send0])
     other_far = [shift(far_up, "y", 1), shift(far_down, "y", -1)]
-    x_send0 = x_part([(kept_x0, got_x0, 0)], x_width, [far_up])
-    other0 = shift(x_send0, "xl", 1)
 
     late_places = [(0, 64, 0, 0), (1, 64, 1, 0), (2, 64, 0, 1), (1, 0, 1, 1), (0, 0, 0, 2), (2, 0, 1, 2)]
-    kept1, sent1 = products([up2, down2, other2], late_places, [b_z, b_x], [x_send0], 3, joined=True)
+    kept1, sent1 = products([up2, down2, other2], late_places, [b_z, b_x], [far_up], 3, joined=True)
     got1 = shift(sent1, "c", 1)
     kept_z2, sent_z2, kept_x2, sent_x2 = products(
         other_far, [(0, 0, 0, 0), (1, 0, 1, 0)], [b_z, b_x], [kept1, got_z0], 1
@@ -293,25 +294,25 @@
     ]
     first = Ring(slots, z_lots, 32, 32, 0, cut)
     done = first.begin(gate([kept_z2]))
-    done = first.rest(done)
     first.hop(0)
     first.hop(1)
     x_send1 = x_part([(kept1, got1, cut), (kept_x2, got_x2, 0)], x_width, [*done, other0])
     other1 = shift(x_send1, "xl", 1)
+    done = first.rest([x_send1])
     x_lots = [
         ((0, 4), [(kept_x0, 64, 0, 0), (got_x0, 64, 0, 0), (other0, 32, 0, 0)]),
         ((4, 7), [(kept1, 64, 0, cut), (got1, 64, 0, cut), (other1, 32, 0, 0)]),
         ((7, 8), [(kept_x2, 64, 0, 0), (got_x2, 64, 0, 0), (other1, 32, 96, 0)]),
     ]
     second = Ring(slots, x_lots, 16, 0, 16, x_width)
-    done = [x_send1]
     for step in STEPS:
         ring, way = (first, second)[step[0] == "x"], "ud".find(step[1])
         if step == "x begin":
             done = second.begin(done)
-            done = second.rest(done)
             second.hop(0)
             second.hop(1)
+        elif step == "x rest":
+            done = second.rest(done)
         elif step == "z end":
             far_sum = add_up(first.parts(0), done)
             from_x = shift(far_sum, "xl", 1)

time: 109 us -> 106 us (0.972)
  waiting for transfers between devices: 37.2 us -> 34.7 us
    ppermute x32 -> x16, starting transfers between devices: 45.9 us -> 16.1 us  [shift(): return lax.ppermute(x, axis, [(i, (i + by) % n) for i in range(n)])]
    ppermute x0 -> x16, starting transfers between devices: none -> 29.6 us  [hop(): self.got[way].append(lax.ppermute(self.sends[way], ('z', 'c'), pairs))]
    ppermute x32 -> x16, waiting for transfers between devices: 37.2 us -> 14.6 us  [shift(): return lax.ppermute(x, axis, [(i, (i + by) % n) for i in range(n)])]
    ppermute x0 -> x16, waiting for transfers between devices: none -> 20.1 us  [hop(): self.got[way].append(lax.ppermute(self.sends[way], ('z', 'c'), pairs))]
    pallas_call x28 -> x29, Pallas kernels: 23.8 us -> 23.5 us  [local(): pl.pallas_call(kernel, in_specs=[SMEM] * len(scalars) + [VMEM] * len(ins)...]
  transfers between devices with their start and end apart: 32 -> 32, of which waited for: 14 -> 13; matrix products, arithmetic and copies ran while one was open for 0% -> 0% of each run, Pallas kernels for 21% -> 21%
where the time goes in v1:
time: 106 us
  starting transfers between devices  45.7 us (43%)
  waiting for transfers between devices  34.7 us (33%)
  Pallas kernels  23.5 us (22%)
  local copies, waits for them, and re-layouts  1.17 us (1%)
    ppermute x16, starting transfers between devices, hop(): self.got[way].append(lax.ppermute(self.sends[way], ('z', 'c'), pairs))  29.6 us
    pallas_call x29, Pallas kernels, local(): pl.pallas_call(kernel, in_specs=[SMEM] * len(scalars) + [VMEM] * len(ins)...  23.5 us
    ppermute x16, waiting for transfers between devices, hop(): self.got[way].append(lax.ppermute(self.sends[way], ('z', 'c'), pairs))  20.1 us
    ppermute x16, starting transfers between devices, shift(): return lax.ppermute(x, axis, [(i, (i + by) % n) for i in range(n)])  16.1 us
    ppermute x16, waiting for transfers between devices, shift(): return lax.ppermute(x, axis, [(i, (i + by) % n) for i in range(n)])  14.6 us
  transfers between devices with their start and end apart: 32, of which 13 were waited for; matrix products, arithmetic and copies ran while one was open for 0% of the time, Pallas kernels for 21%

profile of v1, /device:TPU:4, one launch (start us, length us, event | category | flops | bytes accessed | tf_op | source)
XLA Modules:
  0.0 105.5 jit_solution(7964983790032683110)
XLA Ops:
  1.3 1.7 %collective-permute-start.2 = (f32[128,704]{1,0:T(8,128)S(1)}, f32[128,704]{1,0:T(8,128)S(1)}, u32[]{:S(2)}, u32[]{:S(2)}) collective-permute-start(f32[128,704]{1,0:T(8,128)S(1)} %bitcast.4), channel_id=1, source_target_pairs={{0,2},{2,4},{4,6},{6,0},{1,3},{3,5},{5,7},{7,1},{8,10},{10,12},{12... | collective-permute-start | bytes 1081352 | tf_op jit(solution)/shard_map/ppermute | solution.py:27
  2.9 1.7 %collective-permute-start.1 = (f32[128,704]{1,0:T(8,128)S(1)}, f32[128,704]{1,0:T(8,128)S(1)}, u32[]{:S(2)}, u32[]{:S(2)}) collective-permute-start(f32[128,704]{1,0:T(8,128)S(1)} %bitcast.5), channel_id=1, source_target_pairs={{0,6},{2,0},{4,2},{6,4},{1,7},{3,1},{5,3},{7,5},{8,14},{10,8},{12,... | collective-permute-start | bytes 1081352 | tf_op jit(solution)/shard_map/ppermute | solution.py:27
  4.6 2.2 %collective-permute-start = (f32[128,704]{1,0:T(8,128)S(1)}, f32[128,704]{1,0:T(8,128)S(1)}, u32[]{:S(2)}, u32[]{:S(2)}) collective-permute-start(f32[128,704]{1,0:T(8,128)S(1)} %bitcast.6), channel_id=1, source_target_pairs={{0,1},{1,0},{2,3},{3,2},{4,5},{5,4},{6,7},{7,6},{8,9},{9,8},{10,11... | collective-permute-start | bytes 1081352 | tf_op jit(solution)/shard_map/ppermute | solution.py:27
  6.8 3.5 %shard_map.28 = (bf16[704,1536]{1,0:T(8,128)(2,1)S(1)}, bf16[704,1536]{1,0:T(8,128)(2,1)S(1)}, bf16[704,1280]{1,0:T(8,128)(2,1)S(1)}, bf16[704,1280]{1,0:T(8,128)(2,1)S(1)}) custom-call(f32[704,2816]{1,0:T(8,128)} %refs_0_.1, s32[8]{0:T(128)S(1)} %shift-right-arithmetic_and_fusion.refs_1_.refs_0_), custom_call_target="tpu_custom_call" | custom-call | flops 20000000000 | bytes 1 | tf_op jit(solution)/shard_map/pallas_call | solution.py:44
  10.4 1.9 %shard_map.29 = (f32[256,1280]{1,0:T(8,128)S(1)}, f32[256,1280]{1,0:T(8,128)S(1)}, f32[256,1536]{1,0:T(8,128)S(1)}, f32[256,1536]{1,0:T(8,128)S(1)}) custom-call(f32[128,704]{1,0:T(8,128)S(1)} %bitcast.7, bf16[704,1280]{1,0:T(8,128)(2,1)S(1)} %get-tuple-element.48.refs_1_.refs_3_.refs_5_.refs_4_, ...), custom_call_target="tpu_custom_call" | custom-call | flops 20000000000 | bytes 1 | tf_op jit(solution)/shard_map/pallas_call | solution.py:44
  12.3 1.2 %collective-permute-done.2.refs_2_.refs_0_ = f32[128,704]{1,0:T(8,128)S(1)} collective-permute-done((f32[128,704]{1,0:T(8,128)S(1)}, f32[128,704]{1,0:T(8,128)S(1)}, u32[]{:S(2)}, u32[]{:S(2)}) %collective-permute-start.2) | collective-permute-done | bytes 360480 | tf_op jit(solution)/shard_map/ppermute | solution.py:27
  13.5 3.0 %collective-permute-done.refs_0_.refs_2_ = f32[128,704]{1,0:T(8,128)S(1)} collective-permute-done((f32[128,704]{1,0:T(8,128)S(1)}, f32[128,704]{1,0:T(8,128)S(1)}, u32[]{:S(2)}, u32[]{:S(2)}) %collective-permute-start) | collective-permute-done | bytes 360480 | tf_op jit(solution)/shard_map/ppermute | solution.py:27
  16.9 3.0 %collective-permute-start.5 = (f32[128,704]{1,0:T(8,128)S(1)}, f32[128,704]{1,0:T(8,128)S(1)}, u32[]{:S(2)}, u32[]{:S(2)}) collective-permute-start(f32[128,704]{1,0:T(8,128)S(1)} %get-tuple-element.59), channel_id=1, source_target_pairs={{0,6},{2,0},{4,2},{6,4},{1,7},{3,1},{5,3},{7,5},{8,14},{10,8},{12,... | collective-permute-start | bytes 1081352 | tf_op jit(solution)/shard_map/ppermute | solution.py:27
  20.4 5.2 %shard_map.30 = (f32[256,1280]{1,0:T(8,128)S(1)}, f32[256,1280]{1,0:T(8,128)S(1)}, f32[256,1536]{1,0:T(8,128)S(1)}, f32[256,1536]{1,0:T(8,128)S(1)}) custom-call(f32[128,704]{1,0:T(8,128)S(1)} %collective-permute-done.refs_0_.refs_2_, ...), custom_call_target="tpu_custom_call", output_to_operand_aliasing={{0}: (7, {}), {1}: (8, {}), {2}: (9, {}), {3}: (10, {})} | custom-call | flops 1 | bytes 1 | tf_op jit(solution)/shard_map/pallas_call | solution.py:44
  27.4 3.0 %collective-permute-done.6.refs_3_.refs_2_ = f32[128,704]{1,0:T(8,128)S(1)} collective-permute-done((f32[128,704]{1,0:T(8,128)S(1)}, f32[128,704]{1,0:T(8,128)S(1)}, u32[]{:S(2)}, u32[]{:S(2)}) %collective-permute-start.6) | collective-permute-done | bytes 360480 | tf_op jit(solution)/shard_map/ppermute | solution.py:27
  30.5 1.3 %collective-permute-start.13 = (f32[128,1280]{1,0:T(8,128)S(1)}, f32[128,1280]{1,0:T(8,128)S(1)}, u32[]{:S(2)}, u32[]{:S(2)}) collective-permute-start(f32[128,1280]{1,0:T(8,128)S(1)} %shard_map.33.refs_2_), channel_id=1, source_target_pairs={{0,16},{16,0},{1,17},{17,1},{2,18},{18,2},{3,19},{19,3},{4,20},{20... | collective-permute-start | bytes 1966088 | tf_op jit(solution)/shard_map/ppermute | solution.py:27
  32.3 1.7 %collective-permute-start.9 = (f32[64,704]{1,0:T(8,128)S(1)}, f32[64,704]{1,0:T(8,128)S(1)}, u32[]{:S(2)}, u32[]{:S(2)}) collective-permute-start(f32[64,704]{1,0:T(8,128)S(1)} %get-tuple-element.63.refs_7_), channel_id=1, source_target_pairs={{0,2},{2,4},{4,6},{6,0},{1,3},{3,5},{5,7},{7,1},{8,10},{10,12},{12... | collective-permute-start | bytes 540680 | tf_op jit(solution)/shard_map/ppermute | solution.py:27
  34.1 5.2 %shard_map.35 = (f32[192,2816]{1,0:T(8,128)S(1)}, f32[192,2816]{1,0:T(8,128)S(1)}) custom-call(f32[128,704]{1,0:T(8,128)S(1)} %collective-permute-done.4.refs_1_.refs_0_, f32[128,704]{1,0:T(8,128)S(1)} %collective-permute-done.5.refs_2_.refs_1_, f32[128,704]{1,0:T(8,128)S(1)} %collective-permute-done.6.refs_3_.refs_2_, ...), custom_call_target="tpu_custom_call" | custom-call | flops 20000000000 | bytes 1 | tf_op jit(solution)/shard_map/pallas_call | solution.py:44
  39.4 1.9 %shard_map.36 = (f32[64,1536]{1,0:T(8,128)S(1)}, f32[64,1536]{1,0:T(8,128)S(1)}, f32[64,1280]{1,0:T(8,128)S(1)}, f32[64,1280]{1,0:T(8,128)S(1)}) custom-call(f32[64,704]{1,0:T(8,128)S(1)} %collective-permute-done.9.refs_0_, f32[64,704]{1,0:T(8,128)S(1)} %collective-permute-done.10.refs_1_, bf16[704,1536]{1,0:T(8,128)(2,1)S(1)} %get-tuple-element.50.refs_3_.refs_5_.refs_2_, ...), custom_call_target="tpu_custom_call" | custom-call | flops 20000000000 | bytes 1 | tf_op jit(solution)/shard_map/pallas_call | solution.py:44
  42.0 2.2 %collective-permute-done.11.refs_6_ = f32[64,1536]{1,0:T(8,128)S(1)} collective-permute-done((f32[64,1536]{1,0:T(8,128)S(1)}, f32[64,1536]{1,0:T(8,128)S(1)}, u32[]{:S(2)}, u32[]{:S(2)}) %collective-permute-start.11) | collective-permute-done | bytes 393248 | tf_op jit(solution)/shard_map/ppermute | solution.py:27
  45.0 2.0 %collective-permute-start.15 = (f32[64,1536]{1,0:T(8,128)S(1)}, f32[64,1536]{1,0:T(8,128)S(1)}, u32[]{:S(2)}, u32[]{:S(2)}) collective-permute-start(f32[64,1536]{1,0:T(8,128)S(1)} %get-tuple-element.71.refs_4_), channel_id=1, source_target_pairs={{0,32},{8,232},{32,64},{40,8},{64,96},{72,40},{96,128},{104,72},{1... | collective-permute-start | bytes 1179656 | tf_op jit(solution)/shard_map/ppermute | solution.py:196
  47.0 4.0 %collective-permute-start.14 = (f32[64,1536]{1,0:T(8,128)S(1)}, f32[64,1536]{1,0:T(8,128)S(1)}, u32[]{:S(2)}, u32[]{:S(2)}) collective-permute-start(f32[64,1536]{1,0:T(8,128)S(1)} %get-tuple-element.72.refs_5_), channel_id=1, source_target_pairs={{0,224},{8,40},{32,0},{40,72},{64,32},{72,104},{96,64},{104,136},{... | collective-permute-start | bytes 1179656 | tf_op jit(solution)/shard_map/ppermute | solution.py:196
  52.0 1.4 %shard_map.40 = (f32[64,1536]{1,0:T(8,128)S(1)}, f32[64,1536]{1,0:T(8,128)S(1)}, f32[32,1536]{1,0:T(8,128)S(1)}, f32[64,1536]{1,0:T(8,128)S(1)}, f32[64,1536]{1,...) custom-call(s32[8]{0:T(128)S(1)} %shift-right-arithmetic_and_fusion.refs_1_.refs_0_, ...), custom_call_target="tpu_custom_call" | custom-call | flops 20000000000 | bytes 1 | tf_op jit(solution)/shard_map/pallas_call | solution.py:44
  53.5 5.3 %collective-permute-done.15.refs_0_ = f32[64,1536]{1,0:T(8,128)S(1)} collective-permute-done((f32[64,1536]{1,0:T(8,128)S(1)}, f32[64,1536]{1,0:T(8,128)S(1)}, u32[]{:S(2)}, u32[]{:S(2)}) %collective-permute-start.15) | collective-permute-done | bytes 393248 | tf_op jit(solution)/shard_map/ppermute | solution.py:196
  59.7 4.0 %collective-permute-start.16 = (f32[64,1536]{1,0:T(8,128)S(1)}, f32[64,1536]{1,0:T(8,128)S(1)}, u32[]{:S(2)}, u32[]{:S(2)}) collective-permute-start(f32[64,1536]{1,0:T(8,128)S(1)} %shard_map.42.refs_9_), channel_id=1, source_target_pairs={{0,224},{8,40},{32,0},{40,72},{64,32},{72,104},{96,64},{104,136},{... | collective-permute-start | bytes 1179656 | tf_op jit(solution)/shard_map/ppermute | solution.py:196
  63.7 4.0 %collective-permute-done.18.refs_6_ = f32[128,1280]{1,0:T(8,128)S(1)} collective-permute-done((f32[128,1280]{1,0:T(8,128)S(1)}, f32[128,1280]{1,0:T(8,128)S(1)}, u32[]{:S(2)}, u32[]{:S(2)}) %collective-permute-start.18) | collective-permute-done | bytes 655392 | tf_op jit(solution)/shard_map/ppermute | solution.py:27
  68.5 3.2 %collective-permute-start.21 = (f32[32,1280]{1,0:T(8,128)S(1)}, f32[32,1280]{1,0:T(8,128)S(1)}, u32[]{:S(2)}, u32[]{:S(2)}) collective-permute-start(f32[32,1280]{1,0:T(8,128)S(1)} %get-tuple-element.79.refs_3_), channel_id=1, source_target_pairs={{0,224},{8,40},{32,0},{40,72},{64,32},{72,104},{96,64},{104,136},{... | collective-permute-start | bytes 491528 | tf_op jit(solution)/shard_map/ppermute | solution.py:196
  72.0 3.3 %collective-permute-start.19 = (f32[64,1536]{1,0:T(8,128)S(1)}, f32[64,1536]{1,0:T(8,128)S(1)}, u32[]{:S(2)}, u32[]{:S(2)}) collective-permute-start(f32[64,1536]{1,0:T(8,128)S(1)} %shard_map.45.refs_9_), channel_id=1, source_target_pairs={{0,224},{8,40},{32,0},{40,72},{64,32},{72,104},{96,64},{104,136},{... | collective-permute-start | bytes 1179656 | tf_op jit(solution)/shard_map/ppermute | solution.py:196
  75.3 1.4 %shard_map.46 = (f32[32,1280]{1,0:T(8,128)S(1)}, f32[32,1280]{1,0:T(8,128)S(1)}, f32[16,1280]{1,0:T(8,128)S(1)}, f32[32,1280]{1,0:T(8,128)S(1)}, f32[32,1280]{1,...) custom-call(s32[8]{0:T(128)S(1)} %shift-right-arithmetic_and_fusion.refs_1_.refs_0_, ...), custom_call_target="tpu_custom_call" | custom-call | flops 20000000000 | bytes 1 | tf_op jit(solution)/shard_map/pallas_call | solution.py:44
  76.8 3.3 %collective-permute-start.27 = (f32[32,1280]{1,0:T(8,128)S(1)}, f32[32,1280]{1,0:T(8,128)S(1)}, u32[]{:S(2)}, u32[]{:S(2)}) collective-permute-start(f32[32,1280]{1,0:T(8,128)S(1)} %shard_map.48.refs_2_), channel_id=1, source_target_pairs={{0,224},{8,40},{32,0},{40,72},{64,32},{72,104},{96,64},{104,136},{... | collective-permute-start | bytes 491528 | tf_op jit(solution)/shard_map/ppermute | solution.py:196
  80.1 4.1 %collective-permute-done.20.refs_0_.refs_2_ = f32[64,1536]{1,0:T(8,128)S(1)} collective-permute-done((f32[64,1536]{1,0:T(8,128)S(1)}, f32[64,1536]{1,0:T(8,128)S(1)}, u32[]{:S(2)}, u32[]{:S(2)}) %collective-permute-start.20) | collective-permute-done | bytes 393248 | tf_op jit(solution)/shard_map/ppermute | solution.py:196
  84.8 3.8 %collective-permute-start.23 = (f32[32,1536]{1,0:T(8,128)S(1)}, f32[32,1536]{1,0:T(8,128)S(1)}, u32[]{:S(2)}, u32[]{:S(2)}) collective-permute-start(f32[32,1536]{1,0:T(8,128)S(1)} %shard_map.50.refs_2_), channel_id=1, source_target_pairs={{0,224},{8,40},{32,0},{40,72},{64,32},{72,104},{96,64},{104,136},{... | collective-permute-start | bytes 589832 | tf_op jit(solution)/shard_map/ppermute | solution.py:196
  88.8 3.3 %collective-permute-start.29 = (f32[32,1280]{1,0:T(8,128)S(1)}, f32[32,1280]{1,0:T(8,128)S(1)}, u32[]{:S(2)}, u32[]{:S(2)}) collective-permute-start(f32[32,1280]{1,0:T(8,128)S(1)} %shard_map.52.refs_3_), channel_id=1, source_target_pairs={{0,224},{8,40},{32,0},{40,72},{64,32},{72,104},{96,64},{104,136},{... | collective-permute-start | bytes 491528 | tf_op jit(solution)/shard_map/ppermute | solution.py:196
  93.0 3.8 %collective-permute-done.25.refs_0_.refs_8_ = f32[32,1280]{1,0:T(8,128)S(1)} collective-permute-done((f32[32,1280]{1,0:T(8,128)S(1)}, f32[32,1280]{1,0:T(8,128)S(1)}, u32[]{:S(2)}, u32[]{:S(2)}) %collective-permute-start.25) | collective-permute-done | bytes 163872 | tf_op jit(solution)/shard_map/ppermute | solution.py:196
  96.8 2.3 %collective-permute-start.30 = (f32[16,1280]{1,0:T(8,128)S(1)}, f32[16,1280]{1,0:T(8,128)S(1)}, u32[]{:S(2)}, u32[]{:S(2)}) collective-permute-start(f32[16,1280]{1,0:T(8,128)S(1)} %shard_map.55), channel_id=1, source_target_pairs={{0,224},{8,40},{32,0},{40,72},{64,32},{72,104},{96,64},{104,136},{... | collective-permute-start | bytes 245768 | tf_op jit(solution)/shard_map/ppermute | solution.py:196
  99.1 2.4 %collective-permute-done.30.refs_7_ = f32[16,1280]{1,0:T(8,128)S(1)} collective-permute-done((f32[16,1280]{1,0:T(8,128)S(1)}, f32[16,1280]{1,0:T(8,128)S(1)}, u32[]{:S(2)}, u32[]{:S(2)}) %collective-permute-start.30) | collective-permute-done | bytes 81952 | tf_op jit(solution)/shard_map/ppermute | solution.py:196
  101.5 3.2 %collective-permute-done.28.refs_4_ = f32[16,1280]{1,0:T(8,128)S(1)} collective-permute-done((f32[16,1280]{1,0:T(8,128)S(1)}, f32[16,1280]{1,0:T(8,128)S(1)}, u32[]{:S(2)}, u32[]{:S(2)}) %collective-permute-start.28) | collective-permute-done | bytes 81952 | tf_op jit(solution)/shard_map/ppermute | solution.py:196
  (66 shorter events, 11.8 us)
Async XLA Ops:
  1.3 12.2 %collective-permute-start.2 = (f32[128,704]{1,0:T(8,128)S(1)}, f32[128,704]{1,0:T(8,128)S(1)}, u32[]{:S(2)}, u32[]{:S(2)}) collective-permute-start(f32[128,704]{1,0:T(8,128)S(1)} %bitcast.4), channel_id=1, source_target_pairs={{0,2},{2,4},{4,6},{6,0},{1,3},{3,5},{5,7},{7,1},{8,10},{10,12},{12... | collective-permute-start | bytes 1081352 | tf_op jit(solution)/shard_map/ppermute | solution.py:27
  2.9 10.6 %collective-permute-start.1 = (f32[128,704]{1,0:T(8,128)S(1)}, f32[128,704]{1,0:T(8,128)S(1)}, u32[]{:S(2)}, u32[]{:S(2)}) collective-permute-start(f32[128,704]{1,0:T(8,128)S(1)} %bitcast.5), channel_id=1, source_target_pairs={{0,6},{2,0},{4,2},{6,4},{1,7},{3,1},{5,3},{7,5},{8,14},{10,8},{12,... | collective-permute-start | bytes 1081352 | tf_op jit(solution)/shard_map/ppermute | solution.py:27
  4.6 11.9 %collective-permute-start = (f32[128,704]{1,0:T(8,128)S(1)}, f32[128,704]{1,0:T(8,128)S(1)}, u32[]{:S(2)}, u32[]{:S(2)}) collective-permute-start(f32[128,704]{1,0:T(8,128)S(1)} %bitcast.6), channel_id=1, source_target_pairs={{0,1},{1,0},{2,3},{3,2},{4,5},{5,4},{6,7},{7,6},{8,9},{9,8},{10,11... | collective-permute-start | bytes 1081352 | tf_op jit(solution)/shard_map/ppermute | solution.py:27
  16.6 10.8 %collective-permute-start.4 = (f32[128,704]{1,0:T(8,128)S(1)}, f32[128,704]{1,0:T(8,128)S(1)}, u32[]{:S(2)}, u32[]{:S(2)}) collective-permute-start(f32[128,704]{1,0:T(8,128)S(1)} %get-tuple-element.58), channel_id=1, source_target_pairs={{0,2},{2,4},{4,6},{6,0},{1,3},{3,5},{5,7},{7,1},{8,10},{10,12},{12... | collective-permute-start | bytes 1081352 | tf_op jit(solution)/shard_map/ppermute | solution.py:27
  16.9 10.5 %collective-permute-start.5 = (f32[128,704]{1,0:T(8,128)S(1)}, f32[128,704]{1,0:T(8,128)S(1)}, u32[]{:S(2)}, u32[]{:S(2)}) collective-permute-start(f32[128,704]{1,0:T(8,128)S(1)} %get-tuple-element.59), channel_id=1, source_target_pairs={{0,6},{2,0},{4,2},{6,4},{1,7},{3,1},{5,3},{7,5},{8,14},{10,8},{12,... | collective-permute-start | bytes 1081352 | tf_op jit(solution)/shard_map/ppermute | solution.py:27
  19.9 10.5 %collective-permute-start.6 = (f32[128,704]{1,0:T(8,128)S(1)}, f32[128,704]{1,0:T(8,128)S(1)}, u32[]{:S(2)}, u32[]{:S(2)}) collective-permute-start(f32[128,704]{1,0:T(8,128)S(1)} %get-tuple-element.60), channel_id=1, source_target_pairs={{0,1},{1,0},{2,3},{3,2},{4,5},{5,4},{6,7},{7,6},{8,9},{9,8},{10,11... | collective-permute-start | bytes 1081352 | tf_op jit(solution)/shard_map/ppermute | solution.py:27
  25.6 4.8 %collective-permute-start.7 = (f32[256,1280]{1,0:T(8,128)S(1)}, f32[256,1280]{1,0:T(8,128)S(1)}, u32[]{:S(2)}, u32[]{:S(2)}) collective-permute-start(f32[256,1280]{1,0:T(8,128)S(1)} %get-tuple-element.62), channel_id=1, source_target_pairs={{0,8},{8,0},{1,9},{9,1},{2,10},{10,2},{3,11},{11,3},{4,12},{12,4},... | collective-permute-start | bytes 3932168 | tf_op jit(solution)/shard_map/ppermute | solution.py:27
  25.7 13.7 %collective-permute-start.3 = (f32[256,1536]{1,0:T(8,128)S(1)}, f32[256,1536]{1,0:T(8,128)S(1)}, u32[]{:S(2)}, u32[]{:S(2)}) collective-permute-start(f32[256,1536]{1,0:T(8,128)S(1)} %get-tuple-element.57), channel_id=1, source_target_pairs={{0,8},{8,0},{1,9},{9,1},{2,10},{10,2},{3,11},{11,3},{4,12},{12,4},... | collective-permute-start | bytes 4718600 | tf_op jit(solution)/shard_map/ppermute | solution.py:27
  30.5 20.6 %collective-permute-start.13 = (f32[128,1280]{1,0:T(8,128)S(1)}, f32[128,1280]{1,0:T(8,128)S(1)}, u32[]{:S(2)}, u32[]{:S(2)}) collective-permute-start(f32[128,1280]{1,0:T(8,128)S(1)} %shard_map.33.refs_2_), channel_id=1, source_target_pairs={{0,16},{16,0},{1,17},{17,1},{2,18},{18,2},{3,19},{19,3},{4,20},{20... | collective-permute-start | bytes 1966088 | tf_op jit(solution)/shard_map/ppermute | solution.py:27
  31.8 7.6 %collective-permute-start.10 = (f32[64,704]{1,0:T(8,128)S(1)}, f32[64,704]{1,0:T(8,128)S(1)}, u32[]{:S(2)}, u32[]{:S(2)}) collective-permute-start(f32[64,704]{1,0:T(8,128)S(1)} %get-tuple-element.66), channel_id=1, source_target_pairs={{0,6},{2,0},{4,2},{6,4},{1,7},{3,1},{5,3},{7,5},{8,14},{10,8},{12,... | collective-permute-start | bytes 540680 | tf_op jit(solution)/shard_map/ppermute | solution.py:27
  32.3 7.1 %collective-permute-start.9 = (f32[64,704]{1,0:T(8,128)S(1)}, f32[64,704]{1,0:T(8,128)S(1)}, u32[]{:S(2)}, u32[]{:S(2)}) collective-permute-start(f32[64,704]{1,0:T(8,128)S(1)} %get-tuple-element.63.refs_7_), channel_id=1, source_target_pairs={{0,2},{2,4},{4,6},{6,0},{1,3},{3,5},{5,7},{7,1},{8,10},{10,12},{12... | collective-permute-start | bytes 540680 | tf_op jit(solution)/shard_map/ppermute | solution.py:27
  39.3 4.9 %collective-permute-start.8 = (f32[192,2816]{1,0:T(8,128)S(1)}, f32[192,2816]{1,0:T(8,128)S(1)}, u32[]{:S(2)}, u32[]{:S(2)}) collective-permute-start(f32[192,2816]{1,0:T(8,128)S(1)} %get-tuple-element.65), channel_id=1, source_target_pairs={{0,8},{8,0},{1,9},{9,1},{2,10},{10,2},{3,11},{11,3},{4,12},{12,4},... | collective-permute-start | bytes 6488072 | tf_op jit(solution)/shard_map/ppermute | solution.py:27
  41.3 2.9 %collective-permute-start.11 = (f32[64,1536]{1,0:T(8,128)S(1)}, f32[64,1536]{1,0:T(8,128)S(1)}, u32[]{:S(2)}, u32[]{:S(2)}) collective-permute-start(f32[64,1536]{1,0:T(8,128)S(1)} %get-tuple-element.68), channel_id=1, source_target_pairs={{0,8},{8,0},{1,9},{9,1},{2,10},{10,2},{3,11},{11,3},{4,12},{12,4},... | collective-permute-start | bytes 1179656 | tf_op jit(solution)/shard_map/ppermute | solution.py:27
  41.9 9.2 %collective-permute-start.12 = (f32[64,1280]{1,0:T(8,128)S(1)}, f32[64,1280]{1,0:T(8,128)S(1)}, u32[]{:S(2)}, u32[]{:S(2)}) collective-permute-start(f32[64,1280]{1,0:T(8,128)S(1)} %get-tuple-element.70), channel_id=1, source_target_pairs={{0,8},{8,0},{1,9},{9,1},{2,10},{10,2},{3,11},{11,3},{4,12},{12,4},... | collective-permute-start | bytes 983048 | tf_op jit(solution)/shard_map/ppermute | solution.py:27
  45.0 13.7 %collective-permute-start.15 = (f32[64,1536]{1,0:T(8,128)S(1)}, f32[64,1536]{1,0:T(8,128)S(1)}, u32[]{:S(2)}, u32[]{:S(2)}) collective-permute-start(f32[64,1536]{1,0:T(8,128)S(1)} %get-tuple-element.71.refs_4_), channel_id=1, source_target_pairs={{0,32},{8,232},{32,64},{40,8},{64,96},{72,40},{96,128},{104,72},{1... | collective-permute-start | bytes 1179656 | tf_op jit(solution)/shard_map/ppermute | solution.py:196
  47.0 12.6 %collective-permute-start.14 = (f32[64,1536]{1,0:T(8,128)S(1)}, f32[64,1536]{1,0:T(8,128)S(1)}, u32[]{:S(2)}, u32[]{:S(2)}) collective-permute-start(f32[64,1536]{1,0:T(8,128)S(1)} %get-tuple-element.72.refs_5_), channel_id=1, source_target_pairs={{0,224},{8,40},{32,0},{40,72},{64,32},{72,104},{96,64},{104,136},{... | collective-permute-start | bytes 1179656 | tf_op jit(solution)/shard_map/ppermute | solution.py:196
  51.1 16.5 %collective-permute-start.18 = (f32[128,1280]{1,0:T(8,128)S(1)}, f32[128,1280]{1,0:T(8,128)S(1)}, u32[]{:S(2)}, u32[]{:S(2)}) collective-permute-start(f32[128,1280]{1,0:T(8,128)S(1)} %shard_map.39.refs_7_), channel_id=1, source_target_pairs={{0,16},{16,0},{1,17},{17,1},{2,18},{18,2},{3,19},{19,3},{4,20},{20... | collective-permute-start | bytes 1966088 | tf_op jit(solution)/shard_map/ppermute | solution.py:27
  58.8 13.0 %collective-permute-start.17 = (f32[64,1536]{1,0:T(8,128)S(1)}, f32[64,1536]{1,0:T(8,128)S(1)}, u32[]{:S(2)}, u32[]{:S(2)}) collective-permute-start(f32[64,1536]{1,0:T(8,128)S(1)} %shard_map.41.refs_2_), channel_id=1, source_target_pairs={{0,32},{8,232},{32,64},{40,8},{64,96},{72,40},{96,128},{104,72},{1... | collective-permute-start | bytes 1179656 | tf_op jit(solution)/shard_map/ppermute | solution.py:196
  59.7 12.2 %collective-permute-start.16 = (f32[64,1536]{1,0:T(8,128)S(1)}, f32[64,1536]{1,0:T(8,128)S(1)}, u32[]{:S(2)}, u32[]{:S(2)}) collective-permute-start(f32[64,1536]{1,0:T(8,128)S(1)} %shard_map.42.refs_9_), channel_id=1, source_target_pairs={{0,224},{8,40},{32,0},{40,72},{64,32},{72,104},{96,64},{104,136},{... | collective-permute-start | bytes 1179656 | tf_op jit(solution)/shard_map/ppermute | solution.py:196
  68.4 8.2 %collective-permute-start.22 = (f32[32,1280]{1,0:T(8,128)S(1)}, f32[32,1280]{1,0:T(8,128)S(1)}, u32[]{:S(2)}, u32[]{:S(2)}) collective-permute-start(f32[32,1280]{1,0:T(8,128)S(1)} %get-tuple-element.78.refs_2_), channel_id=1, source_target_pairs={{0,32},{8,232},{32,64},{40,8},{64,96},{72,40},{96,128},{104,72},{1... | collective-permute-start | bytes 491528 | tf_op jit(solution)/shard_map/ppermute | solution.py:196
  68.5 8.2 %collective-permute-start.21 = (f32[32,1280]{1,0:T(8,128)S(1)}, f32[32,1280]{1,0:T(8,128)S(1)}, u32[]{:S(2)}, u32[]{:S(2)}) collective-permute-start(f32[32,1280]{1,0:T(8,128)S(1)} %get-tuple-element.79.refs_3_), channel_id=1, source_target_pairs={{0,224},{8,40},{32,0},{40,72},{64,32},{72,104},{96,64},{104,136},{... | collective-permute-start | bytes 491528 | tf_op jit(solution)/shard_map/ppermute | solution.py:196
  71.8 12.4 %collective-permute-start.20 = (f32[64,1536]{1,0:T(8,128)S(1)}, f32[64,1536]{1,0:T(8,128)S(1)}, u32[]{:S(2)}, u32[]{:S(2)}) collective-permute-start(f32[64,1536]{1,0:T(8,128)S(1)} %shard_map.44.refs_2_), channel_id=1, source_target_pairs={{0,32},{8,232},{32,64},{40,8},{64,96},{72,40},{96,128},{104,72},{1... | collective-permute-start | bytes 1179656 | tf_op jit(solution)/shard_map/ppermute | solution.py:196
  72.0 12.9 %collective-permute-start.19 = (f32[64,1536]{1,0:T(8,128)S(1)}, f32[64,1536]{1,0:T(8,128)S(1)}, u32[]{:S(2)}, u32[]{:S(2)}) collective-permute-start(f32[64,1536]{1,0:T(8,128)S(1)} %shard_map.45.refs_9_), channel_id=1, source_target_pairs={{0,224},{8,40},{32,0},{40,72},{64,32},{72,104},{96,64},{104,136},{... | collective-permute-start | bytes 1179656 | tf_op jit(solution)/shard_map/ppermute | solution.py:196
  76.7 12.0 %collective-permute-start.24 = (f32[32,1280]{1,0:T(8,128)S(1)}, f32[32,1280]{1,0:T(8,128)S(1)}, u32[]{:S(2)}, u32[]{:S(2)}) collective-permute-start(f32[32,1280]{1,0:T(8,128)S(1)} %shard_map.47.refs_2_), channel_id=1, source_target_pairs={{0,32},{8,232},{32,64},{40,8},{64,96},{72,40},{96,128},{104,72},{1... | collective-permute-start | bytes 491528 | tf_op jit(solution)/shard_map/ppermute | solution.py:196
  76.8 12.0 %collective-permute-start.27 = (f32[32,1280]{1,0:T(8,128)S(1)}, f32[32,1280]{1,0:T(8,128)S(1)}, u32[]{:S(2)}, u32[]{:S(2)}) collective-permute-start(f32[32,1280]{1,0:T(8,128)S(1)} %shard_map.48.refs_2_), channel_id=1, source_target_pairs={{0,224},{8,40},{32,0},{40,72},{64,32},{72,104},{96,64},{104,136},{... | collective-permute-start | bytes 491528 | tf_op jit(solution)/shard_map/ppermute | solution.py:196
  84.2 7.9 %collective-permute-start.26 = (f32[32,1536]{1,0:T(8,128)S(1)}, f32[32,1536]{1,0:T(8,128)S(1)}, u32[]{:S(2)}, u32[]{:S(2)}) collective-permute-start(f32[32,1536]{1,0:T(8,128)S(1)} %shard_map.49.refs_2_), channel_id=1, source_target_pairs={{0,32},{8,232},{32,64},{40,8},{64,96},{72,40},{96,128},{104,72},{1... | collective-permute-start | bytes 589832 | tf_op jit(solution)/shard_map/ppermute | solution.py:196
  84.8 14.2 %collective-permute-start.23 = (f32[32,1536]{1,0:T(8,128)S(1)}, f32[32,1536]{1,0:T(8,128)S(1)}, u32[]{:S(2)}, u32[]{:S(2)}) collective-permute-start(f32[32,1536]{1,0:T(8,128)S(1)} %shard_map.50.refs_2_), channel_id=1, source_target_pairs={{0,224},{8,40},{32,0},{40,72},{64,32},{72,104},{96,64},{104,136},{... | collective-permute-start | bytes 589832 | tf_op jit(solution)/shard_map/ppermute | solution.py:196
  88.6 8.1 %collective-permute-start.25 = (f32[32,1280]{1,0:T(8,128)S(1)}, f32[32,1280]{1,0:T(8,128)S(1)}, u32[]{:S(2)}, u32[]{:S(2)}) collective-permute-start(f32[32,1280]{1,0:T(8,128)S(1)} %shard_map.51.refs_2_), channel_id=1, source_target_pairs={{0,32},{8,232},{32,64},{40,8},{64,96},{72,40},{96,128},{104,72},{1... | collective-permute-start | bytes 491528 | tf_op jit(solution)/shard_map/ppermute | solution.py:196
  88.8 8.0 %collective-permute-start.29 = (f32[32,1280]{1,0:T(8,128)S(1)}, f32[32,1280]{1,0:T(8,128)S(1)}, u32[]{:S(2)}, u32[]{:S(2)}) collective-permute-start(f32[32,1280]{1,0:T(8,128)S(1)} %shard_map.52.refs_3_), channel_id=1, source_target_pairs={{0,224},{8,40},{32,0},{40,72},{64,32},{72,104},{96,64},{104,136},{... | collective-permute-start | bytes 491528 | tf_op jit(solution)/shard_map/ppermute | solution.py:196
  92.1 12.6 %collective-permute-start.31 = (f32[32,1536]{1,0:T(8,128)S(1)}, f32[32,1536]{1,0:T(8,128)S(1)}, u32[]{:S(2)}, u32[]{:S(2)}) collective-permute-start(f32[32,1536]{1,0:T(8,128)S(1)} %shard_map.53.refs_2_), channel_id=1, source_target_pairs={{0,16},{16,0},{1,17},{17,1},{2,18},{18,2},{3,19},{19,3},{4,20},{20... | collective-permute-start | bytes 589832 | tf_op jit(solution)/shard_map/ppermute | solution.py:27
  96.8 4.7 %collective-permute-start.30 = (f32[16,1280]{1,0:T(8,128)S(1)}, f32[16,1280]{1,0:T(8,128)S(1)}, u32[]{:S(2)}, u32[]{:S(2)}) collective-permute-start(f32[16,1280]{1,0:T(8,128)S(1)} %shard_map.55), channel_id=1, source_target_pairs={{0,224},{8,40},{32,0},{40,72},{64,32},{72,104},{96,64},{104,136},{... | collective-permute-start | bytes 245768 | tf_op jit(solution)/shard_map/ppermute | solution.py:196
  99.1 5.7 %collective-permute-start.28 = (f32[16,1280]{1,0:T(8,128)S(1)}, f32[16,1280]{1,0:T(8,128)S(1)}, u32[]{:S(2)}, u32[]{:S(2)}) collective-permute-start(f32[16,1280]{1,0:T(8,128)S(1)} %shard_map.54.refs_2_), channel_id=1, source_target_pairs={{0,32},{8,232},{32,64},{40,8},{64,96},{72,40},{96,128},{104,72},{1... | collective-permute-start | bytes 245768 | tf_op jit(solution)/shard_map/ppermute | solution.py:196

commit v2 on v1

--- a/solution.py
+++ b/solution.py
@@ -231,7 +231,7 @@
     return local(body, terms, deps, [((n, width), jnp.float32)])[0]
 
 
-def finish(left, from_x, right_a, right_b):
+def finish(left, from_x, right_a, right_b, deps):
     cut = from_x.shape[1]
 
     def body(ins, outs):
@@ -241,7 +241,7 @@
         outs[0][16:, cut:] = 0.5 * total(6)
 
     shape = (32, cut + right_a[0].shape[1])
-    return local(body, [*left, *right_a, *right_b, from_x], [], [(shape, jnp.float32)], pinned=False)[0]
+    return local(body, [*left, *right_a, *right_b, from_x], deps, [(shape, jnp.float32)], pinned=False)[0]
 
 
 def per_device(amplitudes, integrals):
@@ -320,7 +320,7 @@
         else:
             done = ring.add(way, done)
             ring.hop(way)
-    return finish(first.parts(1), from_x, second.parts(0), second.parts(1))
+    return finish(first.parts(1), from_x, second.parts(0), second.parts(1), gate(done))
 
 
 def solution(mesh):

time: 106 us -> 104 us (0.981)
  waiting for transfers between devices: 34.7 us -> 31.4 us
  starting transfers between devices: 45.7 us -> 46.8 us
    ppermute x16, waiting for transfers between devices: 20.1 us -> 16.8 us  [hop(): self.got[way].append(lax.ppermute(self.sends[way], ('z', 'c'), pairs))]
    ppermute x16, starting transfers between devices: 29.6 us -> 30.7 us  [hop(): self.got[way].append(lax.ppermute(self.sends[way], ('z', 'c'), pairs))]
    pallas_call x29 -> x30, Pallas kernels: 23.5 us -> 23.5 us  [local(): pl.pallas_call(kernel, in_specs=[SMEM] * len(scalars) + [VMEM] * len(ins)...]
  transfers between devices with their start and end apart: 32 -> 32, of which waited for: 13 -> 13; matrix products, arithmetic and copies ran while one was open for 0% -> 0% of each run, Pallas kernels for 21% -> 22%
where the time goes in v2:
time: 104 us; the launch traced here: 103 us
  starting transfers between devices  46.8 us (45%)
  waiting for transfers between devices  31.4 us (30%)
  Pallas kernels  23.5 us (23%)
  local copies, waits for them, and re-layouts  1.17 us (1%)
    ppermute x16, starting transfers between devices, hop(): self.got[way].append(lax.ppermute(self.sends[way], ('z', 'c'), pairs))  30.7 us
    pallas_call x30, Pallas kernels, local(): pl.pallas_call(kernel, in_specs=[SMEM] * len(scalars) + [VMEM] * len(ins)...  23.5 us
    ppermute x16, waiting for transfers between devices, hop(): self.got[way].append(lax.ppermute(self.sends[way], ('z', 'c'), pairs))  16.8 us
    ppermute x16, starting transfers between devices, shift(): return lax.ppermute(x, axis, [(i, (i + by) % n) for i in range(n)])  16.1 us
    ppermute x16, waiting for transfers between devices, shift(): return lax.ppermute(x, axis, [(i, (i + by) % n) for i in range(n)])  14.6 us
  transfers between devices with their start and end apart: 32, of which 13 were waited for; matrix products, arithmetic and copies ran while one was open for 0% of the time, Pallas kernels for 22%

profile of v2, /device:TPU:4, one launch (start us, length us, event | category | flops | bytes accessed | tf_op | source)
XLA Modules:
  0.0 103.3 jit_solution(16284327272462797009)
XLA Ops:
  1.3 1.7 %collective-permute-start.2 = (f32[128,704]{1,0:T(8,128)S(1)}, f32[128,704]{1,0:T(8,128)S(1)}, u32[]{:S(2)}, u32[]{:S(2)}) collective-permute-start(f32[128,704]{1,0:T(8,128)S(1)} %bitcast.4), channel_id=1, source_target_pairs={{0,2},{2,4},{4,6},{6,0},{1,3},{3,5},{5,7},{7,1},{8,10},{10,12},{12... | collective-permute-start | bytes 1081352 | tf_op jit(solution)/shard_map/ppermute | solution.py:27
  2.9 1.7 %collective-permute-start.1 = (f32[128,704]{1,0:T(8,128)S(1)}, f32[128,704]{1,0:T(8,128)S(1)}, u32[]{:S(2)}, u32[]{:S(2)}) collective-permute-start(f32[128,704]{1,0:T(8,128)S(1)} %bitcast.5), channel_id=1, source_target_pairs={{0,6},{2,0},{4,2},{6,4},{1,7},{3,1},{5,3},{7,5},{8,14},{10,8},{12,... | collective-permute-start | bytes 1081352 | tf_op jit(solution)/shard_map/ppermute | solution.py:27
  4.6 2.2 %collective-permute-start = (f32[128,704]{1,0:T(8,128)S(1)}, f32[128,704]{1,0:T(8,128)S(1)}, u32[]{:S(2)}, u32[]{:S(2)}) collective-permute-start(f32[128,704]{1,0:T(8,128)S(1)} %bitcast.6), channel_id=1, source_target_pairs={{0,1},{1,0},{2,3},{3,2},{4,5},{5,4},{6,7},{7,6},{8,9},{9,8},{10,11... | collective-permute-start | bytes 1081352 | tf_op jit(solution)/shard_map/ppermute | solution.py:27
  6.8 3.5 %shard_map.28 = (bf16[704,1536]{1,0:T(8,128)(2,1)S(1)}, bf16[704,1536]{1,0:T(8,128)(2,1)S(1)}, bf16[704,1280]{1,0:T(8,128)(2,1)S(1)}, bf16[704,1280]{1,0:T(8,128)(2,1)S(1)}) custom-call(f32[704,2816]{1,0:T(8,128)} %refs_0_.1, s32[8]{0:T(128)S(1)} %shift-right-arithmetic_and_fusion.refs_1_.refs_0_), custom_call_target="tpu_custom_call" | custom-call | flops 20000000000 | bytes 1 | tf_op jit(solution)/shard_map/pallas_call | solution.py:44
  10.4 1.9 %shard_map.29 = (f32[256,1280]{1,0:T(8,128)S(1)}, f32[256,1280]{1,0:T(8,128)S(1)}, f32[256,1536]{1,0:T(8,128)S(1)}, f32[256,1536]{1,0:T(8,128)S(1)}) custom-call(f32[128,704]{1,0:T(8,128)S(1)} %bitcast.7, bf16[704,1280]{1,0:T(8,128)(2,1)S(1)} %get-tuple-element.48.refs_1_.refs_3_.refs_5_.refs_4_, ...), custom_call_target="tpu_custom_call" | custom-call | flops 20000000000 | bytes 1 | tf_op jit(solution)/shard_map/pallas_call | solution.py:44
  12.3 1.2 %collective-permute-done.2.refs_2_.refs_0_ = f32[128,704]{1,0:T(8,128)S(1)} collective-permute-done((f32[128,704]{1,0:T(8,128)S(1)}, f32[128,704]{1,0:T(8,128)S(1)}, u32[]{:S(2)}, u32[]{:S(2)}) %collective-permute-start.2) | collective-permute-done | bytes 360480 | tf_op jit(solution)/shard_map/ppermute | solution.py:27
  13.5 3.0 %collective-permute-done.refs_0_.refs_2_ = f32[128,704]{1,0:T(8,128)S(1)} collective-permute-done((f32[128,704]{1,0:T(8,128)S(1)}, f32[128,704]{1,0:T(8,128)S(1)}, u32[]{:S(2)}, u32[]{:S(2)}) %collective-permute-start) | collective-permute-done | bytes 360480 | tf_op jit(solution)/shard_map/ppermute | solution.py:27
  16.9 3.0 %collective-permute-start.5 = (f32[128,704]{1,0:T(8,128)S(1)}, f32[128,704]{1,0:T(8,128)S(1)}, u32[]{:S(2)}, u32[]{:S(2)}) collective-permute-start(f32[128,704]{1,0:T(8,128)S(1)} %get-tuple-element.59), channel_id=1, source_target_pairs={{0,6},{2,0},{4,2},{6,4},{1,7},{3,1},{5,3},{7,5},{8,14},{10,8},{12,... | collective-permute-start | bytes 1081352 | tf_op jit(solution)/shard_map/ppermute | solution.py:27
  20.4 5.2 %shard_map.30 = (f32[256,1280]{1,0:T(8,128)S(1)}, f32[256,1280]{1,0:T(8,128)S(1)}, f32[256,1536]{1,0:T(8,128)S(1)}, f32[256,1536]{1,0:T(8,128)S(1)}) custom-call(f32[128,704]{1,0:T(8,128)S(1)} %collective-permute-done.refs_0_.refs_2_, ...), custom_call_target="tpu_custom_call", output_to_operand_aliasing={{0}: (7, {}), {1}: (8, {}), {2}: (9, {}), {3}: (10, {})} | custom-call | flops 1 | bytes 1 | tf_op jit(solution)/shard_map/pallas_call | solution.py:44
  26.2 1.2 %collective-permute-done.4.refs_1_.refs_0_ = f32[128,704]{1,0:T(8,128)S(1)} collective-permute-done((f32[128,704]{1,0:T(8,128)S(1)}, f32[128,704]{1,0:T(8,128)S(1)}, u32[]{:S(2)}, u32[]{:S(2)}) %collective-permute-start.4) | collective-permute-done | bytes 360480 | tf_op jit(solution)/shard_map/ppermute | solution.py:27
  27.4 3.0 %collective-permute-done.6.refs_3_.refs_2_ = f32[128,704]{1,0:T(8,128)S(1)} collective-permute-done((f32[128,704]{1,0:T(8,128)S(1)}, f32[128,704]{1,0:T(8,128)S(1)}, u32[]{:S(2)}, u32[]{:S(2)}) %collective-permute-start.6) | collective-permute-done | bytes 360480 | tf_op jit(solution)/shard_map/ppermute | solution.py:27
  30.5 1.3 %collective-permute-start.13 = (f32[128,1280]{1,0:T(8,128)S(1)}, f32[128,1280]{1,0:T(8,128)S(1)}, u32[]{:S(2)}, u32[]{:S(2)}) collective-permute-start(f32[128,1280]{1,0:T(8,128)S(1)} %shard_map.33.refs_2_), channel_id=1, source_target_pairs={{0,16},{16,0},{1,17},{17,1},{2,18},{18,2},{3,19},{19,3},{4,20},{20... | collective-permute-start | bytes 1966088 | tf_op jit(solution)/shard_map/ppermute | solution.py:27
  32.3 1.7 %collective-permute-start.9 = (f32[64,704]{1,0:T(8,128)S(1)}, f32[64,704]{1,0:T(8,128)S(1)}, u32[]{:S(2)}, u32[]{:S(2)}) collective-permute-start(f32[64,704]{1,0:T(8,128)S(1)} %get-tuple-element.63.refs_7_), channel_id=1, source_target_pairs={{0,2},{2,4},{4,6},{6,0},{1,3},{3,5},{5,7},{7,1},{8,10},{10,12},{12... | collective-permute-start | bytes 540680 | tf_op jit(solution)/shard_map/ppermute | solution.py:27
  34.1 5.2 %shard_map.35 = (f32[192,2816]{1,0:T(8,128)S(1)}, f32[192,2816]{1,0:T(8,128)S(1)}) custom-call(f32[128,704]{1,0:T(8,128)S(1)} %collective-permute-done.4.refs_1_.refs_0_, f32[128,704]{1,0:T(8,128)S(1)} %collective-permute-done.5.refs_2_.refs_1_, f32[128,704]{1,0:T(8,128)S(1)} %collective-permute-done.6.refs_3_.refs_2_, ...), custom_call_target="tpu_custom_call" | custom-call | flops 20000000000 | bytes 1 | tf_op jit(solution)/shard_map/pallas_call | solution.py:44
  39.4 1.9 %shard_map.36 = (f32[64,1536]{1,0:T(8,128)S(1)}, f32[64,1536]{1,0:T(8,128)S(1)}, f32[64,1280]{1,0:T(8,128)S(1)}, f32[64,1280]{1,0:T(8,128)S(1)}) custom-call(f32[64,704]{1,0:T(8,128)S(1)} %collective-permute-done.9.refs_0_, f32[64,704]{1,0:T(8,128)S(1)} %collective-permute-done.10.refs_1_, bf16[704,1536]{1,0:T(8,128)(2,1)S(1)} %get-tuple-element.50.refs_3_.refs_5_.refs_2_, ...), custom_call_target="tpu_custom_call" | custom-call | flops 20000000000 | bytes 1 | tf_op jit(solution)/shard_map/pallas_call | solution.py:44
  42.0 2.2 %collective-permute-done.11.refs_6_ = f32[64,1536]{1,0:T(8,128)S(1)} collective-permute-done((f32[64,1536]{1,0:T(8,128)S(1)}, f32[64,1536]{1,0:T(8,128)S(1)}, u32[]{:S(2)}, u32[]{:S(2)}) %collective-permute-start.11) | collective-permute-done | bytes 393248 | tf_op jit(solution)/shard_map/ppermute | solution.py:27
  45.0 2.0 %collective-permute-start.15 = (f32[64,1536]{1,0:T(8,128)S(1)}, f32[64,1536]{1,0:T(8,128)S(1)}, u32[]{:S(2)}, u32[]{:S(2)}) collective-permute-start(f32[64,1536]{1,0:T(8,128)S(1)} %get-tuple-element.71.refs_4_), channel_id=1, source_target_pairs={{0,32},{8,232},{32,64},{40,8},{64,96},{72,40},{96,128},{104,72},{1... | collective-permute-start | bytes 1179656 | tf_op jit(solution)/shard_map/ppermute | solution.py:196
  47.0 4.0 %collective-permute-start.14 = (f32[64,1536]{1,0:T(8,128)S(1)}, f32[64,1536]{1,0:T(8,128)S(1)}, u32[]{:S(2)}, u32[]{:S(2)}) collective-permute-start(f32[64,1536]{1,0:T(8,128)S(1)} %get-tuple-element.72.refs_5_), channel_id=1, source_target_pairs={{0,224},{8,40},{32,0},{40,72},{64,32},{72,104},{96,64},{104,136},{... | collective-permute-start | bytes 1179656 | tf_op jit(solution)/shard_map/ppermute | solution.py:196
  52.0 1.4 %shard_map.40 = (f32[64,1536]{1,0:T(8,128)S(1)}, f32[64,1536]{1,0:T(8,128)S(1)}, f32[32,1536]{1,0:T(8,128)S(1)}, f32[64,1536]{1,0:T(8,128)S(1)}, f32[64,1536]{1,...) custom-call(s32[8]{0:T(128)S(1)} %shift-right-arithmetic_and_fusion.refs_1_.refs_0_, ...), custom_call_target="tpu_custom_call" | custom-call | flops 20000000000 | bytes 1 | tf_op jit(solution)/shard_map/pallas_call | solution.py:44
  53.5 5.3 %collective-permute-done.15.refs_0_ = f32[64,1536]{1,0:T(8,128)S(1)} collective-permute-done((f32[64,1536]{1,0:T(8,128)S(1)}, f32[64,1536]{1,0:T(8,128)S(1)}, u32[]{:S(2)}, u32[]{:S(2)}) %collective-permute-start.15) | collective-permute-done | bytes 393248 | tf_op jit(solution)/shard_map/ppermute | solution.py:196
  59.7 4.0 %collective-permute-start.16 = (f32[64,1536]{1,0:T(8,128)S(1)}, f32[64,1536]{1,0:T(8,128)S(1)}, u32[]{:S(2)}, u32[]{:S(2)}) collective-permute-start(f32[64,1536]{1,0:T(8,128)S(1)} %shard_map.42.refs_9_), channel_id=1, source_target_pairs={{0,224},{8,40},{32,0},{40,72},{64,32},{72,104},{96,64},{104,136},{... | collective-permute-start | bytes 1179656 | tf_op jit(solution)/shard_map/ppermute | solution.py:196
  63.7 4.0 %collective-permute-done.18.refs_6_ = f32[128,1280]{1,0:T(8,128)S(1)} collective-permute-done((f32[128,1280]{1,0:T(8,128)S(1)}, f32[128,1280]{1,0:T(8,128)S(1)}, u32[]{:S(2)}, u32[]{:S(2)}) %collective-permute-start.18) | collective-permute-done | bytes 655392 | tf_op jit(solution)/shard_map/ppermute | solution.py:27
  68.5 3.2 %collective-permute-start.21 = (f32[32,1280]{1,0:T(8,128)S(1)}, f32[32,1280]{1,0:T(8,128)S(1)}, u32[]{:S(2)}, u32[]{:S(2)}) collective-permute-start(f32[32,1280]{1,0:T(8,128)S(1)} %get-tuple-element.79.refs_3_), channel_id=1, source_target_pairs={{0,224},{8,40},{32,0},{40,72},{64,32},{72,104},{96,64},{104,136},{... | collective-permute-start | bytes 491528 | tf_op jit(solution)/shard_map/ppermute | solution.py:196
  72.0 3.3 %collective-permute-start.19 = (f32[64,1536]{1,0:T(8,128)S(1)}, f32[64,1536]{1,0:T(8,128)S(1)}, u32[]{:S(2)}, u32[]{:S(2)}) collective-permute-start(f32[64,1536]{1,0:T(8,128)S(1)} %shard_map.45.refs_9_), channel_id=1, source_target_pairs={{0,224},{8,40},{32,0},{40,72},{64,32},{72,104},{96,64},{104,136},{... | collective-permute-start | bytes 1179656 | tf_op jit(solution)/shard_map/ppermute | solution.py:196
  75.3 1.4 %shard_map.46 = (f32[32,1280]{1,0:T(8,128)S(1)}, f32[32,1280]{1,0:T(8,128)S(1)}, f32[16,1280]{1,0:T(8,128)S(1)}, f32[32,1280]{1,0:T(8,128)S(1)}, f32[32,1280]{1,...) custom-call(s32[8]{0:T(128)S(1)} %shift-right-arithmetic_and_fusion.refs_1_.refs_0_, ...), custom_call_target="tpu_custom_call" | custom-call | flops 20000000000 | bytes 1 | tf_op jit(solution)/shard_map/pallas_call | solution.py:44
  76.8 3.3 %collective-permute-start.27 = (f32[32,1280]{1,0:T(8,128)S(1)}, f32[32,1280]{1,0:T(8,128)S(1)}, u32[]{:S(2)}, u32[]{:S(2)}) collective-permute-start(f32[32,1280]{1,0:T(8,128)S(1)} %shard_map.48.refs_2_), channel_id=1, source_target_pairs={{0,224},{8,40},{32,0},{40,72},{64,32},{72,104},{96,64},{104,136},{... | collective-permute-start | bytes 491528 | tf_op jit(solution)/shard_map/ppermute | solution.py:196
  80.1 4.1 %collective-permute-done.20.refs_0_.refs_2_ = f32[64,1536]{1,0:T(8,128)S(1)} collective-permute-done((f32[64,1536]{1,0:T(8,128)S(1)}, f32[64,1536]{1,0:T(8,128)S(1)}, u32[]{:S(2)}, u32[]{:S(2)}) %collective-permute-start.20) | collective-permute-done | bytes 393248 | tf_op jit(solution)/shard_map/ppermute | solution.py:196
  84.8 3.8 %collective-permute-start.23 = (f32[32,1536]{1,0:T(8,128)S(1)}, f32[32,1536]{1,0:T(8,128)S(1)}, u32[]{:S(2)}, u32[]{:S(2)}) collective-permute-start(f32[32,1536]{1,0:T(8,128)S(1)} %shard_map.50.refs_2_), channel_id=1, source_target_pairs={{0,224},{8,40},{32,0},{40,72},{64,32},{72,104},{96,64},{104,136},{... | collective-permute-start | bytes 589832 | tf_op jit(solution)/shard_map/ppermute | solution.py:196
  88.8 3.3 %collective-permute-start.29 = (f32[32,1280]{1,0:T(8,128)S(1)}, f32[32,1280]{1,0:T(8,128)S(1)}, u32[]{:S(2)}, u32[]{:S(2)}) collective-permute-start(f32[32,1280]{1,0:T(8,128)S(1)} %shard_map.52.refs_3_), channel_id=1, source_target_pairs={{0,224},{8,40},{32,0},{40,72},{64,32},{72,104},{96,64},{104,136},{... | collective-permute-start | bytes 491528 | tf_op jit(solution)/shard_map/ppermute | solution.py:196
  93.0 3.8 %collective-permute-done.25.refs_0_.refs_8_ = f32[32,1280]{1,0:T(8,128)S(1)} collective-permute-done((f32[32,1280]{1,0:T(8,128)S(1)}, f32[32,1280]{1,0:T(8,128)S(1)}, u32[]{:S(2)}, u32[]{:S(2)}) %collective-permute-start.25) | collective-permute-done | bytes 163872 | tf_op jit(solution)/shard_map/ppermute | solution.py:196
  96.9 3.3 %collective-permute-start.30 = (f32[16,1280]{1,0:T(8,128)S(1)}, f32[16,1280]{1,0:T(8,128)S(1)}, u32[]{:S(2)}, u32[]{:S(2)}) collective-permute-start(f32[16,1280]{1,0:T(8,128)S(1)} %shard_map.55.refs_0_), channel_id=1, source_target_pairs={{0,224},{8,40},{32,0},{40,72},{64,32},{72,104},{96,64},{104,136},{... | collective-permute-start | bytes 245768 | tf_op jit(solution)/shard_map/ppermute | solution.py:196
  100.2 2.1 %collective-permute-done.30.refs_7_ = f32[16,1280]{1,0:T(8,128)S(1)} collective-permute-done((f32[16,1280]{1,0:T(8,128)S(1)}, f32[16,1280]{1,0:T(8,128)S(1)}, u32[]{:S(2)}, u32[]{:S(2)}) %collective-permute-start.30) | collective-permute-done | bytes 81952 | tf_op jit(solution)/shard_map/ppermute | solution.py:196
  (67 shorter events, 11.0 us)
Async XLA Ops:
  1.3 12.2 %collective-permute-start.2 = (f32[128,704]{1,0:T(8,128)S(1)}, f32[128,704]{1,0:T(8,128)S(1)}, u32[]{:S(2)}, u32[]{:S(2)}) collective-permute-start(f32[128,704]{1,0:T(8,128)S(1)} %bitcast.4), channel_id=1, source_target_pairs={{0,2},{2,4},{4,6},{6,0},{1,3},{3,5},{5,7},{7,1},{8,10},{10,12},{12... | collective-permute-start | bytes 1081352 | tf_op jit(solution)/shard_map/ppermute | solution.py:27
  2.9 10.6 %collective-permute-start.1 = (f32[128,704]{1,0:T(8,128)S(1)}, f32[128,704]{1,0:T(8,128)S(1)}, u32[]{:S(2)}, u32[]{:S(2)}) collective-permute-start(f32[128,704]{1,0:T(8,128)S(1)} %bitcast.5), channel_id=1, source_target_pairs={{0,6},{2,0},{4,2},{6,4},{1,7},{3,1},{5,3},{7,5},{8,14},{10,8},{12,... | collective-permute-start | bytes 1081352 | tf_op jit(solution)/shard_map/ppermute | solution.py:27
  4.6 11.9 %collective-permute-start = (f32[128,704]{1,0:T(8,128)S(1)}, f32[128,704]{1,0:T(8,128)S(1)}, u32[]{:S(2)}, u32[]{:S(2)}) collective-permute-start(f32[128,704]{1,0:T(8,128)S(1)} %bitcast.6), channel_id=1, source_target_pairs={{0,1},{1,0},{2,3},{3,2},{4,5},{5,4},{6,7},{7,6},{8,9},{9,8},{10,11... | collective-permute-start | bytes 1081352 | tf_op jit(solution)/shard_map/ppermute | solution.py:27
  16.6 10.8 %collective-permute-start.4 = (f32[128,704]{1,0:T(8,128)S(1)}, f32[128,704]{1,0:T(8,128)S(1)}, u32[]{:S(2)}, u32[]{:S(2)}) collective-permute-start(f32[128,704]{1,0:T(8,128)S(1)} %get-tuple-element.58), channel_id=1, source_target_pairs={{0,2},{2,4},{4,6},{6,0},{1,3},{3,5},{5,7},{7,1},{8,10},{10,12},{12... | collective-permute-start | bytes 1081352 | tf_op jit(solution)/shard_map/ppermute | solution.py:27
  16.9 10.5 %collective-permute-start.5 = (f32[128,704]{1,0:T(8,128)S(1)}, f32[128,704]{1,0:T(8,128)S(1)}, u32[]{:S(2)}, u32[]{:S(2)}) collective-permute-start(f32[128,704]{1,0:T(8,128)S(1)} %get-tuple-element.59), channel_id=1, source_target_pairs={{0,6},{2,0},{4,2},{6,4},{1,7},{3,1},{5,3},{7,5},{8,14},{10,8},{12,... | collective-permute-start | bytes 1081352 | tf_op jit(solution)/shard_map/ppermute | solution.py:27
  19.9 10.5 %collective-permute-start.6 = (f32[128,704]{1,0:T(8,128)S(1)}, f32[128,704]{1,0:T(8,128)S(1)}, u32[]{:S(2)}, u32[]{:S(2)}) collective-permute-start(f32[128,704]{1,0:T(8,128)S(1)} %get-tuple-element.60), channel_id=1, source_target_pairs={{0,1},{1,0},{2,3},{3,2},{4,5},{5,4},{6,7},{7,6},{8,9},{9,8},{10,11... | collective-permute-start | bytes 1081352 | tf_op jit(solution)/shard_map/ppermute | solution.py:27
  25.6 4.8 %collective-permute-start.7 = (f32[256,1280]{1,0:T(8,128)S(1)}, f32[256,1280]{1,0:T(8,128)S(1)}, u32[]{:S(2)}, u32[]{:S(2)}) collective-permute-start(f32[256,1280]{1,0:T(8,128)S(1)} %get-tuple-element.62), channel_id=1, source_target_pairs={{0,8},{8,0},{1,9},{9,1},{2,10},{10,2},{3,11},{11,3},{4,12},{12,4},... | collective-permute-start | bytes 3932168 | tf_op jit(solution)/shard_map/ppermute | solution.py:27
  25.7 13.7 %collective-permute-start.3 = (f32[256,1536]{1,0:T(8,128)S(1)}, f32[256,1536]{1,0:T(8,128)S(1)}, u32[]{:S(2)}, u32[]{:S(2)}) collective-permute-start(f32[256,1536]{1,0:T(8,128)S(1)} %get-tuple-element.57), channel_id=1, source_target_pairs={{0,8},{8,0},{1,9},{9,1},{2,10},{10,2},{3,11},{11,3},{4,12},{12,4},... | collective-permute-start | bytes 4718600 | tf_op jit(solution)/shard_map/ppermute | solution.py:27
  30.5 20.6 %collective-permute-start.13 = (f32[128,1280]{1,0:T(8,128)S(1)}, f32[128,1280]{1,0:T(8,128)S(1)}, u32[]{:S(2)}, u32[]{:S(2)}) collective-permute-start(f32[128,1280]{1,0:T(8,128)S(1)} %shard_map.33.refs_2_), channel_id=1, source_target_pairs={{0,16},{16,0},{1,17},{17,1},{2,18},{18,2},{3,19},{19,3},{4,20},{20... | collective-permute-start | bytes 1966088 | tf_op jit(solution)/shard_map/ppermute | solution.py:27
  31.8 7.6 %collective-permute-start.10 = (f32[64,704]{1,0:T(8,128)S(1)}, f32[64,704]{1,0:T(8,128)S(1)}, u32[]{:S(2)}, u32[]{:S(2)}) collective-permute-start(f32[64,704]{1,0:T(8,128)S(1)} %get-tuple-element.66), channel_id=1, source_target_pairs={{0,6},{2,0},{4,2},{6,4},{1,7},{3,1},{5,3},{7,5},{8,14},{10,8},{12,... | collective-permute-start | bytes 540680 | tf_op jit(solution)/shard_map/ppermute | solution.py:27
  32.3 7.1 %collective-permute-start.9 = (f32[64,704]{1,0:T(8,128)S(1)}, f32[64,704]{1,0:T(8,128)S(1)}, u32[]{:S(2)}, u32[]{:S(2)}) collective-permute-start(f32[64,704]{1,0:T(8,128)S(1)} %get-tuple-element.63.refs_7_), channel_id=1, source_target_pairs={{0,2},{2,4},{4,6},{6,0},{1,3},{3,5},{5,7},{7,1},{8,10},{10,12},{12... | collective-permute-start | bytes 540680 | tf_op jit(solution)/shard_map/ppermute | solution.py:27
  39.3 4.9 %collective-permute-start.8 = (f32[192,2816]{1,0:T(8,128)S(1)}, f32[192,2816]{1,0:T(8,128)S(1)}, u32[]{:S(2)}, u32[]{:S(2)}) collective-permute-start(f32[192,2816]{1,0:T(8,128)S(1)} %get-tuple-element.65), channel_id=1, source_target_pairs={{0,8},{8,0},{1,9},{9,1},{2,10},{10,2},{3,11},{11,3},{4,12},{12,4},... | collective-permute-start | bytes 6488072 | tf_op jit(solution)/shard_map/ppermute | solution.py:27
  41.3 2.9 %collective-permute-start.11 = (f32[64,1536]{1,0:T(8,128)S(1)}, f32[64,1536]{1,0:T(8,128)S(1)}, u32[]{:S(2)}, u32[]{:S(2)}) collective-permute-start(f32[64,1536]{1,0:T(8,128)S(1)} %get-tuple-element.68), channel_id=1, source_target_pairs={{0,8},{8,0},{1,9},{9,1},{2,10},{10,2},{3,11},{11,3},{4,12},{12,4},... | collective-permute-start | bytes 1179656 | tf_op jit(solution)/shard_map/ppermute | solution.py:27
  41.9 9.2 %collective-permute-start.12 = (f32[64,1280]{1,0:T(8,128)S(1)}, f32[64,1280]{1,0:T(8,128)S(1)}, u32[]{:S(2)}, u32[]{:S(2)}) collective-permute-start(f32[64,1280]{1,0:T(8,128)S(1)} %get-tuple-element.70), channel_id=1, source_target_pairs={{0,8},{8,0},{1,9},{9,1},{2,10},{10,2},{3,11},{11,3},{4,12},{12,4},... | collective-permute-start | bytes 983048 | tf_op jit(solution)/shard_map/ppermute | solution.py:27
  45.0 13.7 %collective-permute-start.15 = (f32[64,1536]{1,0:T(8,128)S(1)}, f32[64,1536]{1,0:T(8,128)S(1)}, u32[]{:S(2)}, u32[]{:S(2)}) collective-permute-start(f32[64,1536]{1,0:T(8,128)S(1)} %get-tuple-element.71.refs_4_), channel_id=1, source_target_pairs={{0,32},{8,232},{32,64},{40,8},{64,96},{72,40},{96,128},{104,72},{1... | collective-permute-start | bytes 1179656 | tf_op jit(solution)/shard_map/ppermute | solution.py:196
  47.0 12.6 %collective-permute-start.14 = (f32[64,1536]{1,0:T(8,128)S(1)}, f32[64,1536]{1,0:T(8,128)S(1)}, u32[]{:S(2)}, u32[]{:S(2)}) collective-permute-start(f32[64,1536]{1,0:T(8,128)S(1)} %get-tuple-element.72.refs_5_), channel_id=1, source_target_pairs={{0,224},{8,40},{32,0},{40,72},{64,32},{72,104},{96,64},{104,136},{... | collective-permute-start | bytes 1179656 | tf_op jit(solution)/shard_map/ppermute | solution.py:196
  51.1 16.5 %collective-permute-start.18 = (f32[128,1280]{1,0:T(8,128)S(1)}, f32[128,1280]{1,0:T(8,128)S(1)}, u32[]{:S(2)}, u32[]{:S(2)}) collective-permute-start(f32[128,1280]{1,0:T(8,128)S(1)} %shard_map.39.refs_7_), channel_id=1, source_target_pairs={{0,16},{16,0},{1,17},{17,1},{2,18},{18,2},{3,19},{19,3},{4,20},{20... | collective-permute-start | bytes 1966088 | tf_op jit(solution)/shard_map/ppermute | solution.py:27
  58.8 13.0 %collective-permute-start.17 = (f32[64,1536]{1,0:T(8,128)S(1)}, f32[64,1536]{1,0:T(8,128)S(1)}, u32[]{:S(2)}, u32[]{:S(2)}) collective-permute-start(f32[64,1536]{1,0:T(8,128)S(1)} %shard_map.41.refs_2_), channel_id=1, source_target_pairs={{0,32},{8,232},{32,64},{40,8},{64,96},{72,40},{96,128},{104,72},{1... | collective-permute-start | bytes 1179656 | tf_op jit(solution)/shard_map/ppermute | solution.py:196
  59.7 12.2 %collective-permute-start.16 = (f32[64,1536]{1,0:T(8,128)S(1)}, f32[64,1536]{1,0:T(8,128)S(1)}, u32[]{:S(2)}, u32[]{:S(2)}) collective-permute-start(f32[64,1536]{1,0:T(8,128)S(1)} %shard_map.42.refs_9_), channel_id=1, source_target_pairs={{0,224},{8,40},{32,0},{40,72},{64,32},{72,104},{96,64},{104,136},{... | collective-permute-start | bytes 1179656 | tf_op jit(solution)/shard_map/ppermute | solution.py:196
  68.4 8.2 %collective-permute-start.22 = (f32[32,1280]{1,0:T(8,128)S(1)}, f32[32,1280]{1,0:T(8,128)S(1)}, u32[]{:S(2)}, u32[]{:S(2)}) collective-permute-start(f32[32,1280]{1,0:T(8,128)S(1)} %get-tuple-element.78.refs_2_), channel_id=1, source_target_pairs={{0,32},{8,232},{32,64},{40,8},{64,96},{72,40},{96,128},{104,72},{1... | collective-permute-start | bytes 491528 | tf_op jit(solution)/shard_map/ppermute | solution.py:196
  68.5 8.2 %collective-permute-start.21 = (f32[32,1280]{1,0:T(8,128)S(1)}, f32[32,1280]{1,0:T(8,128)S(1)}, u32[]{:S(2)}, u32[]{:S(2)}) collective-permute-start(f32[32,1280]{1,0:T(8,128)S(1)} %get-tuple-element.79.refs_3_), channel_id=1, source_target_pairs={{0,224},{8,40},{32,0},{40,72},{64,32},{72,104},{96,64},{104,136},{... | collective-permute-start | bytes 491528 | tf_op jit(solution)/shard_map/ppermute | solution.py:196
  71.8 12.4 %collective-permute-start.20 = (f32[64,1536]{1,0:T(8,128)S(1)}, f32[64,1536]{1,0:T(8,128)S(1)}, u32[]{:S(2)}, u32[]{:S(2)}) collective-permute-start(f32[64,1536]{1,0:T(8,128)S(1)} %shard_map.44.refs_2_), channel_id=1, source_target_pairs={{0,32},{8,232},{32,64},{40,8},{64,96},{72,40},{96,128},{104,72},{1... | collective-permute-start | bytes 1179656 | tf_op jit(solution)/shard_map/ppermute | solution.py:196
  72.0 12.9 %collective-permute-start.19 = (f32[64,1536]{1,0:T(8,128)S(1)}, f32[64,1536]{1,0:T(8,128)S(1)}, u32[]{:S(2)}, u32[]{:S(2)}) collective-permute-start(f32[64,1536]{1,0:T(8,128)S(1)} %shard_map.45.refs_9_), channel_id=1, source_target_pairs={{0,224},{8,40},{32,0},{40,72},{64,32},{72,104},{96,64},{104,136},{... | collective-permute-start | bytes 1179656 | tf_op jit(solution)/shard_map/ppermute | solution.py:196
  76.7 12.0 %collective-permute-start.24 = (f32[32,1280]{1,0:T(8,128)S(1)}, f32[32,1280]{1,0:T(8,128)S(1)}, u32[]{:S(2)}, u32[]{:S(2)}) collective-permute-start(f32[32,1280]{1,0:T(8,128)S(1)} %shard_map.47.refs_2_), channel_id=1, source_target_pairs={{0,32},{8,232},{32,64},{40,8},{64,96},{72,40},{96,128},{104,72},{1... | collective-permute-start | bytes 491528 | tf_op jit(solution)/shard_map/ppermute | solution.py:196
  76.8 12.0 %collective-permute-start.27 = (f32[32,1280]{1,0:T(8,128)S(1)}, f32[32,1280]{1,0:T(8,128)S(1)}, u32[]{:S(2)}, u32[]{:S(2)}) collective-permute-start(f32[32,1280]{1,0:T(8,128)S(1)} %shard_map.48.refs_2_), channel_id=1, source_target_pairs={{0,224},{8,40},{32,0},{40,72},{64,32},{72,104},{96,64},{104,136},{... | collective-permute-start | bytes 491528 | tf_op jit(solution)/shard_map/ppermute | solution.py:196
  84.2 7.9 %collective-permute-start.26 = (f32[32,1536]{1,0:T(8,128)S(1)}, f32[32,1536]{1,0:T(8,128)S(1)}, u32[]{:S(2)}, u32[]{:S(2)}) collective-permute-start(f32[32,1536]{1,0:T(8,128)S(1)} %shard_map.49.refs_2_), channel_id=1, source_target_pairs={{0,32},{8,232},{32,64},{40,8},{64,96},{72,40},{96,128},{104,72},{1... | collective-permute-start | bytes 589832 | tf_op jit(solution)/shard_map/ppermute | solution.py:196
  84.8 15.4 %collective-permute-start.23 = (f32[32,1536]{1,0:T(8,128)S(1)}, f32[32,1536]{1,0:T(8,128)S(1)}, u32[]{:S(2)}, u32[]{:S(2)}) collective-permute-start(f32[32,1536]{1,0:T(8,128)S(1)} %shard_map.50.refs_2_), channel_id=1, source_target_pairs={{0,224},{8,40},{32,0},{40,72},{64,32},{72,104},{96,64},{104,136},{... | collective-permute-start | bytes 589832 | tf_op jit(solution)/shard_map/ppermute | solution.py:196
  88.6 8.1 %collective-permute-start.25 = (f32[32,1280]{1,0:T(8,128)S(1)}, f32[32,1280]{1,0:T(8,128)S(1)}, u32[]{:S(2)}, u32[]{:S(2)}) collective-permute-start(f32[32,1280]{1,0:T(8,128)S(1)} %shard_map.51.refs_2_), channel_id=1, source_target_pairs={{0,32},{8,232},{32,64},{40,8},{64,96},{72,40},{96,128},{104,72},{1... | collective-permute-start | bytes 491528 | tf_op jit(solution)/shard_map/ppermute | solution.py:196
  88.8 8.1 %collective-permute-start.29 = (f32[32,1280]{1,0:T(8,128)S(1)}, f32[32,1280]{1,0:T(8,128)S(1)}, u32[]{:S(2)}, u32[]{:S(2)}) collective-permute-start(f32[32,1280]{1,0:T(8,128)S(1)} %shard_map.52.refs_3_), channel_id=1, source_target_pairs={{0,224},{8,40},{32,0},{40,72},{64,32},{72,104},{96,64},{104,136},{... | collective-permute-start | bytes 491528 | tf_op jit(solution)/shard_map/ppermute | solution.py:196
  92.1 10.4 %collective-permute-start.31 = (f32[32,1536]{1,0:T(8,128)S(1)}, f32[32,1536]{1,0:T(8,128)S(1)}, u32[]{:S(2)}, u32[]{:S(2)}) collective-permute-start(f32[32,1536]{1,0:T(8,128)S(1)} %shard_map.53.refs_2_), channel_id=1, source_target_pairs={{0,16},{16,0},{1,17},{17,1},{2,18},{18,2},{3,19},{19,3},{4,20},{20... | collective-permute-start | bytes 589832 | tf_op jit(solution)/shard_map/ppermute | solution.py:27
  96.8 5.7 %collective-permute-start.28 = (f32[16,1280]{1,0:T(8,128)S(1)}, f32[16,1280]{1,0:T(8,128)S(1)}, u32[]{:S(2)}, u32[]{:S(2)}) collective-permute-start(f32[16,1280]{1,0:T(8,128)S(1)} %shard_map.54.refs_2_), channel_id=1, source_target_pairs={{0,32},{8,232},{32,64},{40,8},{64,96},{72,40},{96,128},{104,72},{1... | collective-permute-start | bytes 245768 | tf_op jit(solution)/shard_map/ppermute | solution.py:196
  96.9 5.3 %collective-permute-start.30 = (f32[16,1280]{1,0:T(8,128)S(1)}, f32[16,1280]{1,0:T(8,128)S(1)}, u32[]{:S(2)}, u32[]{:S(2)}) collective-permute-start(f32[16,1280]{1,0:T(8,128)S(1)} %shard_map.55.refs_0_), channel_id=1, source_target_pairs={{0,224},{8,40},{32,0},{40,72},{64,32},{72,104},{96,64},{104,136},{... | collective-permute-start | bytes 245768 | tf_op jit(solution)/shard_map/ppermute | solution.py:196

commit v3 on v2

--- a/solution.py
+++ b/solution.py
@@ -58,8 +58,8 @@
     return high, (x - high.astype(jnp.float32)).astype(jnp.bfloat16)
 
 
-def tile(i, first=0):
-    return pl.ds(pl.multiple_of(first + i * TILE, 128), TILE)
+def tile(i, first=0, size=TILE):
+    return pl.ds(pl.multiple_of(first + i * size, 128), size)
 
 
 def split_columns(b, sets, deps):
@@ -171,12 +171,12 @@
                 def write(first, lot):
                     starts = [pl.multiple_of((s - first) * stride + (row + low), n) for _, stride, row, _ in lot]
 
-                    @pl.loop(0, width // TILE)
+                    @pl.loop(0, 2)
                     def _(i):
                         total = 0.0
                         for (v, _, _, col), start in zip(lot, starts):
-                            total = total + refs[where(v)][pl.ds(start, n), tile(i, col)]
-                        out_refs[out][at : at + n, tile(i)] = total
+                            total = total + refs[where(v)][pl.ds(start, n), tile(i, col, width // 2)]
+                        out_refs[out][at : at + n, tile(i, 0, width // 2)] = total
 
                 for (first, end), lot in self.lots:
                     pl.when((s >= first) & (s < end))(functools.partial(write, first, lot))

time: 104 us -> 104 us (level)
  transfers between devices with their start and end apart: 32 -> 32, of which waited for: 13 -> 13; matrix products, arithmetic and copies ran while one was open for 0% -> 0% of each run, Pallas kernels for 22% -> 21%
where the time goes in v3:
time: 104 us; the launch traced here: 103 us
  starting transfers between devices  46.8 us (45%)
  waiting for transfers between devices  32 us (31%)
  Pallas kernels  22.7 us (22%)
  local copies, waits for them, and re-layouts  1.17 us (1%)
    ppermute x16, starting transfers between devices, hop(): self.got[way].append(lax.ppermute(self.sends[way], ('z', 'c'), pairs))  30.7 us
    pallas_call x30, Pallas kernels, local(): pl.pallas_call(kernel, in_specs=[SMEM] * len(scalars) + [VMEM] * len(ins)...  22.7 us
    ppermute x16, waiting for transfers between devices, hop(): self.got[way].append(lax.ppermute(self.sends[way], ('z', 'c'), pairs))  17.4 us
    ppermute x16, starting transfers between devices, shift(): return lax.ppermute(x, axis, [(i, (i + by) % n) for i in range(n)])  16.1 us
    ppermute x16, waiting for transfers between devices, shift(): return lax.ppermute(x, axis, [(i, (i + by) % n) for i in range(n)])  14.6 us
  transfers between devices with their start and end apart: 32, of which 13 were waited for; matrix products, arithmetic and copies ran while one was open for 0% of the time, Pallas kernels for 21%

profile of v3, /device:TPU:4, one launch (start us, length us, event | category | flops | bytes accessed | tf_op | source)
XLA Modules:
  0.0 103.2 jit_solution(3459430929349031996)
XLA Ops:
  0.0 1.1 %copy.9 = f32[128,704]{1,0:T(8,128)S(1)} copy(f32[128,704]{0,1:T(8,128)} %param.2) | data formatting | bytes 720896 | tf_op args[0]
  1.3 1.7 %collective-permute-start.2 = (f32[128,704]{1,0:T(8,128)S(1)}, f32[128,704]{1,0:T(8,128)S(1)}, u32[]{:S(2)}, u32[]{:S(2)}) collective-permute-start(f32[128,704]{1,0:T(8,128)S(1)} %bitcast.4), channel_id=1, source_target_pairs={{0,2},{2,4},{4,6},{6,0},{1,3},{3,5},{5,7},{7,1},{8,10},{10,12},{12... | collective-permute-start | bytes 1081352 | tf_op jit(solution)/shard_map/ppermute | solution.py:27
  2.9 1.7 %collective-permute-start.1 = (f32[128,704]{1,0:T(8,128)S(1)}, f32[128,704]{1,0:T(8,128)S(1)}, u32[]{:S(2)}, u32[]{:S(2)}) collective-permute-start(f32[128,704]{1,0:T(8,128)S(1)} %bitcast.5), channel_id=1, source_target_pairs={{0,6},{2,0},{4,2},{6,4},{1,7},{3,1},{5,3},{7,5},{8,14},{10,8},{12,... | collective-permute-start | bytes 1081352 | tf_op jit(solution)/shard_map/ppermute | solution.py:27
  4.6 2.2 %collective-permute-start = (f32[128,704]{1,0:T(8,128)S(1)}, f32[128,704]{1,0:T(8,128)S(1)}, u32[]{:S(2)}, u32[]{:S(2)}) collective-permute-start(f32[128,704]{1,0:T(8,128)S(1)} %bitcast.6), channel_id=1, source_target_pairs={{0,1},{1,0},{2,3},{3,2},{4,5},{5,4},{6,7},{7,6},{8,9},{9,8},{10,11... | collective-permute-start | bytes 1081352 | tf_op jit(solution)/shard_map/ppermute | solution.py:27
  6.8 3.5 %shard_map.28 = (bf16[704,1536]{1,0:T(8,128)(2,1)S(1)}, bf16[704,1536]{1,0:T(8,128)(2,1)S(1)}, bf16[704,1280]{1,0:T(8,128)(2,1)S(1)}, bf16[704,1280]{1,0:T(8,128)(2,1)S(1)}) custom-call(f32[704,2816]{1,0:T(8,128)} %refs_0_.1, s32[8]{0:T(128)S(1)} %shift-right-arithmetic_and_fusion.refs_1_.refs_0_), custom_call_target="tpu_custom_call" | custom-call | flops 20000000000 | bytes 1 | tf_op jit(solution)/shard_map/pallas_call | solution.py:44
  10.4 1.9 %shard_map.29 = (f32[256,1280]{1,0:T(8,128)S(1)}, f32[256,1280]{1,0:T(8,128)S(1)}, f32[256,1536]{1,0:T(8,128)S(1)}, f32[256,1536]{1,0:T(8,128)S(1)}) custom-call(f32[128,704]{1,0:T(8,128)S(1)} %bitcast.7, bf16[704,1280]{1,0:T(8,128)(2,1)S(1)} %get-tuple-element.48.refs_1_.refs_3_.refs_5_.refs_4_, ...), custom_call_target="tpu_custom_call" | custom-call | flops 20000000000 | bytes 1 | tf_op jit(solution)/shard_map/pallas_call | solution.py:44
  12.3 1.2 %collective-permute-done.2.refs_2_.refs_0_ = f32[128,704]{1,0:T(8,128)S(1)} collective-permute-done((f32[128,704]{1,0:T(8,128)S(1)}, f32[128,704]{1,0:T(8,128)S(1)}, u32[]{:S(2)}, u32[]{:S(2)}) %collective-permute-start.2) | collective-permute-done | bytes 360480 | tf_op jit(solution)/shard_map/ppermute | solution.py:27
  13.5 3.0 %collective-permute-done.refs_0_.refs_2_ = f32[128,704]{1,0:T(8,128)S(1)} collective-permute-done((f32[128,704]{1,0:T(8,128)S(1)}, f32[128,704]{1,0:T(8,128)S(1)}, u32[]{:S(2)}, u32[]{:S(2)}) %collective-permute-start) | collective-permute-done | bytes 360480 | tf_op jit(solution)/shard_map/ppermute | solution.py:27
  16.9 3.0 %collective-permute-start.5 = (f32[128,704]{1,0:T(8,128)S(1)}, f32[128,704]{1,0:T(8,128)S(1)}, u32[]{:S(2)}, u32[]{:S(2)}) collective-permute-start(f32[128,704]{1,0:T(8,128)S(1)} %get-tuple-element.59), channel_id=1, source_target_pairs={{0,6},{2,0},{4,2},{6,4},{1,7},{3,1},{5,3},{7,5},{8,14},{10,8},{12,... | collective-permute-start | bytes 1081352 | tf_op jit(solution)/shard_map/ppermute | solution.py:27
  20.4 5.2 %shard_map.30 = (f32[256,1280]{1,0:T(8,128)S(1)}, f32[256,1280]{1,0:T(8,128)S(1)}, f32[256,1536]{1,0:T(8,128)S(1)}, f32[256,1536]{1,0:T(8,128)S(1)}) custom-call(f32[128,704]{1,0:T(8,128)S(1)} %collective-permute-done.refs_0_.refs_2_, ...), custom_call_target="tpu_custom_call", output_to_operand_aliasing={{0}: (7, {}), {1}: (8, {}), {2}: (9, {}), {3}: (10, {})} | custom-call | flops 1 | bytes 1 | tf_op jit(solution)/shard_map/pallas_call | solution.py:44
  26.2 1.2 %collective-permute-done.4.refs_1_.refs_0_ = f32[128,704]{1,0:T(8,128)S(1)} collective-permute-done((f32[128,704]{1,0:T(8,128)S(1)}, f32[128,704]{1,0:T(8,128)S(1)}, u32[]{:S(2)}, u32[]{:S(2)}) %collective-permute-start.4) | collective-permute-done | bytes 360480 | tf_op jit(solution)/shard_map/ppermute | solution.py:27
  27.4 3.0 %collective-permute-done.6.refs_3_.refs_2_ = f32[128,704]{1,0:T(8,128)S(1)} collective-permute-done((f32[128,704]{1,0:T(8,128)S(1)}, f32[128,704]{1,0:T(8,128)S(1)}, u32[]{:S(2)}, u32[]{:S(2)}) %collective-permute-start.6) | collective-permute-done | bytes 360480 | tf_op jit(solution)/shard_map/ppermute | solution.py:27
  30.5 1.3 %collective-permute-start.13 = (f32[128,1280]{1,0:T(8,128)S(1)}, f32[128,1280]{1,0:T(8,128)S(1)}, u32[]{:S(2)}, u32[]{:S(2)}) collective-permute-start(f32[128,1280]{1,0:T(8,128)S(1)} %shard_map.33.refs_2_), channel_id=1, source_target_pairs={{0,16},{16,0},{1,17},{17,1},{2,18},{18,2},{3,19},{19,3},{4,20},{20... | collective-permute-start | bytes 1966088 | tf_op jit(solution)/shard_map/ppermute | solution.py:27
  32.3 1.7 %collective-permute-start.9 = (f32[64,704]{1,0:T(8,128)S(1)}, f32[64,704]{1,0:T(8,128)S(1)}, u32[]{:S(2)}, u32[]{:S(2)}) collective-permute-start(f32[64,704]{1,0:T(8,128)S(1)} %get-tuple-element.63.refs_7_), channel_id=1, source_target_pairs={{0,2},{2,4},{4,6},{6,0},{1,3},{3,5},{5,7},{7,1},{8,10},{10,12},{12... | collective-permute-start | bytes 540680 | tf_op jit(solution)/shard_map/ppermute | solution.py:27
  34.1 5.2 %shard_map.35 = (f32[192,2816]{1,0:T(8,128)S(1)}, f32[192,2816]{1,0:T(8,128)S(1)}) custom-call(f32[128,704]{1,0:T(8,128)S(1)} %collective-permute-done.4.refs_1_.refs_0_, f32[128,704]{1,0:T(8,128)S(1)} %collective-permute-done.5.refs_2_.refs_1_, f32[128,704]{1,0:T(8,128)S(1)} %collective-permute-done.6.refs_3_.refs_2_, ...), custom_call_target="tpu_custom_call" | custom-call | flops 20000000000 | bytes 1 | tf_op jit(solution)/shard_map/pallas_call | solution.py:44
  39.4 1.9 %shard_map.36 = (f32[64,1536]{1,0:T(8,128)S(1)}, f32[64,1536]{1,0:T(8,128)S(1)}, f32[64,1280]{1,0:T(8,128)S(1)}, f32[64,1280]{1,0:T(8,128)S(1)}) custom-call(f32[64,704]{1,0:T(8,128)S(1)} %collective-permute-done.9.refs_0_, f32[64,704]{1,0:T(8,128)S(1)} %collective-permute-done.10.refs_1_, bf16[704,1536]{1,0:T(8,128)(2,1)S(1)} %get-tuple-element.50.refs_3_.refs_5_.refs_2_, ...), custom_call_target="tpu_custom_call" | custom-call | flops 20000000000 | bytes 1 | tf_op jit(solution)/shard_map/pallas_call | solution.py:44
  42.0 2.2 %collective-permute-done.11.refs_6_ = f32[64,1536]{1,0:T(8,128)S(1)} collective-permute-done((f32[64,1536]{1,0:T(8,128)S(1)}, f32[64,1536]{1,0:T(8,128)S(1)}, u32[]{:S(2)}, u32[]{:S(2)}) %collective-permute-start.11) | collective-permute-done | bytes 393248 | tf_op jit(solution)/shard_map/ppermute | solution.py:27
  45.0 2.0 %collective-permute-start.15 = (f32[64,1536]{1,0:T(8,128)S(1)}, f32[64,1536]{1,0:T(8,128)S(1)}, u32[]{:S(2)}, u32[]{:S(2)}) collective-permute-start(f32[64,1536]{1,0:T(8,128)S(1)} %get-tuple-element.71.refs_4_), channel_id=1, source_target_pairs={{0,32},{8,232},{32,64},{40,8},{64,96},{72,40},{96,128},{104,72},{1... | collective-permute-start | bytes 1179656 | tf_op jit(solution)/shard_map/ppermute | solution.py:196
  46.9 4.0 %collective-permute-start.14 = (f32[64,1536]{1,0:T(8,128)S(1)}, f32[64,1536]{1,0:T(8,128)S(1)}, u32[]{:S(2)}, u32[]{:S(2)}) collective-permute-start(f32[64,1536]{1,0:T(8,128)S(1)} %get-tuple-element.72.refs_5_), channel_id=1, source_target_pairs={{0,224},{8,40},{32,0},{40,72},{64,32},{72,104},{96,64},{104,136},{... | collective-permute-start | bytes 1179656 | tf_op jit(solution)/shard_map/ppermute | solution.py:196
  52.0 1.1 %shard_map.40 = (f32[64,1536]{1,0:T(8,128)S(1)}, f32[64,1536]{1,0:T(8,128)S(1)}, f32[32,1536]{1,0:T(8,128)S(1)}, f32[64,1536]{1,0:T(8,128)S(1)}, f32[64,1536]{1,...) custom-call(s32[8]{0:T(128)S(1)} %shift-right-arithmetic_and_fusion.refs_1_.refs_0_, ...), custom_call_target="tpu_custom_call" | custom-call | flops 20000000000 | bytes 1 | tf_op jit(solution)/shard_map/pallas_call | solution.py:44
  53.1 5.6 %collective-permute-done.15.refs_0_ = f32[64,1536]{1,0:T(8,128)S(1)} collective-permute-done((f32[64,1536]{1,0:T(8,128)S(1)}, f32[64,1536]{1,0:T(8,128)S(1)}, u32[]{:S(2)}, u32[]{:S(2)}) %collective-permute-start.15) | collective-permute-done | bytes 393248 | tf_op jit(solution)/shard_map/ppermute | solution.py:196
  59.6 4.0 %collective-permute-start.16 = (f32[64,1536]{1,0:T(8,128)S(1)}, f32[64,1536]{1,0:T(8,128)S(1)}, u32[]{:S(2)}, u32[]{:S(2)}) collective-permute-start(f32[64,1536]{1,0:T(8,128)S(1)} %shard_map.42.refs_9_), channel_id=1, source_target_pairs={{0,224},{8,40},{32,0},{40,72},{64,32},{72,104},{96,64},{104,136},{... | collective-permute-start | bytes 1179656 | tf_op jit(solution)/shard_map/ppermute | solution.py:196
  63.6 4.0 %collective-permute-done.18.refs_6_ = f32[128,1280]{1,0:T(8,128)S(1)} collective-permute-done((f32[128,1280]{1,0:T(8,128)S(1)}, f32[128,1280]{1,0:T(8,128)S(1)}, u32[]{:S(2)}, u32[]{:S(2)}) %collective-permute-start.18) | collective-permute-done | bytes 655392 | tf_op jit(solution)/shard_map/ppermute | solution.py:27
  68.4 3.2 %collective-permute-start.21 = (f32[32,1280]{1,0:T(8,128)S(1)}, f32[32,1280]{1,0:T(8,128)S(1)}, u32[]{:S(2)}, u32[]{:S(2)}) collective-permute-start(f32[32,1280]{1,0:T(8,128)S(1)} %get-tuple-element.79.refs_3_), channel_id=1, source_target_pairs={{0,224},{8,40},{32,0},{40,72},{64,32},{72,104},{96,64},{104,136},{... | collective-permute-start | bytes 491528 | tf_op jit(solution)/shard_map/ppermute | solution.py:196
  71.8 3.3 %collective-permute-start.19 = (f32[64,1536]{1,0:T(8,128)S(1)}, f32[64,1536]{1,0:T(8,128)S(1)}, u32[]{:S(2)}, u32[]{:S(2)}) collective-permute-start(f32[64,1536]{1,0:T(8,128)S(1)} %shard_map.45.refs_9_), channel_id=1, source_target_pairs={{0,224},{8,40},{32,0},{40,72},{64,32},{72,104},{96,64},{104,136},{... | collective-permute-start | bytes 1179656 | tf_op jit(solution)/shard_map/ppermute | solution.py:196
  76.3 3.3 %collective-permute-start.27 = (f32[32,1280]{1,0:T(8,128)S(1)}, f32[32,1280]{1,0:T(8,128)S(1)}, u32[]{:S(2)}, u32[]{:S(2)}) collective-permute-start(f32[32,1280]{1,0:T(8,128)S(1)} %shard_map.48.refs_2_), channel_id=1, source_target_pairs={{0,224},{8,40},{32,0},{40,72},{64,32},{72,104},{96,64},{104,136},{... | collective-permute-start | bytes 491528 | tf_op jit(solution)/shard_map/ppermute | solution.py:196
  79.6 4.4 %collective-permute-done.20.refs_0_.refs_2_ = f32[64,1536]{1,0:T(8,128)S(1)} collective-permute-done((f32[64,1536]{1,0:T(8,128)S(1)}, f32[64,1536]{1,0:T(8,128)S(1)}, u32[]{:S(2)}, u32[]{:S(2)}) %collective-permute-start.20) | collective-permute-done | bytes 393248 | tf_op jit(solution)/shard_map/ppermute | solution.py:196
  84.7 3.8 %collective-permute-start.23 = (f32[32,1536]{1,0:T(8,128)S(1)}, f32[32,1536]{1,0:T(8,128)S(1)}, u32[]{:S(2)}, u32[]{:S(2)}) collective-permute-start(f32[32,1536]{1,0:T(8,128)S(1)} %shard_map.50.refs_2_), channel_id=1, source_target_pairs={{0,224},{8,40},{32,0},{40,72},{64,32},{72,104},{96,64},{104,136},{... | collective-permute-start | bytes 589832 | tf_op jit(solution)/shard_map/ppermute | solution.py:196
  88.6 3.3 %collective-permute-start.29 = (f32[32,1280]{1,0:T(8,128)S(1)}, f32[32,1280]{1,0:T(8,128)S(1)}, u32[]{:S(2)}, u32[]{:S(2)}) collective-permute-start(f32[32,1280]{1,0:T(8,128)S(1)} %shard_map.52.refs_3_), channel_id=1, source_target_pairs={{0,224},{8,40},{32,0},{40,72},{64,32},{72,104},{96,64},{104,136},{... | collective-permute-start | bytes 491528 | tf_op jit(solution)/shard_map/ppermute | solution.py:196
  92.8 3.8 %collective-permute-done.25.refs_0_.refs_8_ = f32[32,1280]{1,0:T(8,128)S(1)} collective-permute-done((f32[32,1280]{1,0:T(8,128)S(1)}, f32[32,1280]{1,0:T(8,128)S(1)}, u32[]{:S(2)}, u32[]{:S(2)}) %collective-permute-start.25) | collective-permute-done | bytes 163872 | tf_op jit(solution)/shard_map/ppermute | solution.py:196
  96.7 3.3 %collective-permute-start.30 = (f32[16,1280]{1,0:T(8,128)S(1)}, f32[16,1280]{1,0:T(8,128)S(1)}, u32[]{:S(2)}, u32[]{:S(2)}) collective-permute-start(f32[16,1280]{1,0:T(8,128)S(1)} %shard_map.55.refs_0_), channel_id=1, source_target_pairs={{0,224},{8,40},{32,0},{40,72},{64,32},{72,104},{96,64},{104,136},{... | collective-permute-start | bytes 245768 | tf_op jit(solution)/shard_map/ppermute | solution.py:196
  100.0 2.1 %collective-permute-done.30.refs_7_ = f32[16,1280]{1,0:T(8,128)S(1)} collective-permute-done((f32[16,1280]{1,0:T(8,128)S(1)}, f32[16,1280]{1,0:T(8,128)S(1)}, u32[]{:S(2)}, u32[]{:S(2)}) %collective-permute-start.30) | collective-permute-done | bytes 81952 | tf_op jit(solution)/shard_map/ppermute | solution.py:196
  (67 shorter events, 10.7 us)
Async XLA Ops:
  1.3 12.2 %collective-permute-start.2 = (f32[128,704]{1,0:T(8,128)S(1)}, f32[128,704]{1,0:T(8,128)S(1)}, u32[]{:S(2)}, u32[]{:S(2)}) collective-permute-start(f32[128,704]{1,0:T(8,128)S(1)} %bitcast.4), channel_id=1, source_target_pairs={{0,2},{2,4},{4,6},{6,0},{1,3},{3,5},{5,7},{7,1},{8,10},{10,12},{12... | collective-permute-start | bytes 1081352 | tf_op jit(solution)/shard_map/ppermute | solution.py:27
  2.9 10.6 %collective-permute-start.1 = (f32[128,704]{1,0:T(8,128)S(1)}, f32[128,704]{1,0:T(8,128)S(1)}, u32[]{:S(2)}, u32[]{:S(2)}) collective-permute-start(f32[128,704]{1,0:T(8,128)S(1)} %bitcast.5), channel_id=1, source_target_pairs={{0,6},{2,0},{4,2},{6,4},{1,7},{3,1},{5,3},{7,5},{8,14},{10,8},{12,... | collective-permute-start | bytes 1081352 | tf_op jit(solution)/shard_map/ppermute | solution.py:27
  4.6 11.9 %collective-permute-start = (f32[128,704]{1,0:T(8,128)S(1)}, f32[128,704]{1,0:T(8,128)S(1)}, u32[]{:S(2)}, u32[]{:S(2)}) collective-permute-start(f32[128,704]{1,0:T(8,128)S(1)} %bitcast.6), channel_id=1, source_target_pairs={{0,1},{1,0},{2,3},{3,2},{4,5},{5,4},{6,7},{7,6},{8,9},{9,8},{10,11... | collective-permute-start | bytes 1081352 | tf_op jit(solution)/shard_map/ppermute | solution.py:27
  16.6 10.8 %collective-permute-start.4 = (f32[128,704]{1,0:T(8,128)S(1)}, f32[128,704]{1,0:T(8,128)S(1)}, u32[]{:S(2)}, u32[]{:S(2)}) collective-permute-start(f32[128,704]{1,0:T(8,128)S(1)} %get-tuple-element.58), channel_id=1, source_target_pairs={{0,2},{2,4},{4,6},{6,0},{1,3},{3,5},{5,7},{7,1},{8,10},{10,12},{12... | collective-permute-start | bytes 1081352 | tf_op jit(solution)/shard_map/ppermute | solution.py:27
  16.9 10.5 %collective-permute-start.5 = (f32[128,704]{1,0:T(8,128)S(1)}, f32[128,704]{1,0:T(8,128)S(1)}, u32[]{:S(2)}, u32[]{:S(2)}) collective-permute-start(f32[128,704]{1,0:T(8,128)S(1)} %get-tuple-element.59), channel_id=1, source_target_pairs={{0,6},{2,0},{4,2},{6,4},{1,7},{3,1},{5,3},{7,5},{8,14},{10,8},{12,... | collective-permute-start | bytes 1081352 | tf_op jit(solution)/shard_map/ppermute | solution.py:27
  19.9 10.5 %collective-permute-start.6 = (f32[128,704]{1,0:T(8,128)S(1)}, f32[128,704]{1,0:T(8,128)S(1)}, u32[]{:S(2)}, u32[]{:S(2)}) collective-permute-start(f32[128,704]{1,0:T(8,128)S(1)} %get-tuple-element.60), channel_id=1, source_target_pairs={{0,1},{1,0},{2,3},{3,2},{4,5},{5,4},{6,7},{7,6},{8,9},{9,8},{10,11... | collective-permute-start | bytes 1081352 | tf_op jit(solution)/shard_map/ppermute | solution.py:27
  25.6 4.8 %collective-permute-start.7 = (f32[256,1280]{1,0:T(8,128)S(1)}, f32[256,1280]{1,0:T(8,128)S(1)}, u32[]{:S(2)}, u32[]{:S(2)}) collective-permute-start(f32[256,1280]{1,0:T(8,128)S(1)} %get-tuple-element.62), channel_id=1, source_target_pairs={{0,8},{8,0},{1,9},{9,1},{2,10},{10,2},{3,11},{11,3},{4,12},{12,4},... | collective-permute-start | bytes 3932168 | tf_op jit(solution)/shard_map/ppermute | solution.py:27
  25.7 13.7 %collective-permute-start.3 = (f32[256,1536]{1,0:T(8,128)S(1)}, f32[256,1536]{1,0:T(8,128)S(1)}, u32[]{:S(2)}, u32[]{:S(2)}) collective-permute-start(f32[256,1536]{1,0:T(8,128)S(1)} %get-tuple-element.57), channel_id=1, source_target_pairs={{0,8},{8,0},{1,9},{9,1},{2,10},{10,2},{3,11},{11,3},{4,12},{12,4},... | collective-permute-start | bytes 4718600 | tf_op jit(solution)/shard_map/ppermute | solution.py:27
  30.5 20.5 %collective-permute-start.13 = (f32[128,1280]{1,0:T(8,128)S(1)}, f32[128,1280]{1,0:T(8,128)S(1)}, u32[]{:S(2)}, u32[]{:S(2)}) collective-permute-start(f32[128,1280]{1,0:T(8,128)S(1)} %shard_map.33.refs_2_), channel_id=1, source_target_pairs={{0,16},{16,0},{1,17},{17,1},{2,18},{18,2},{3,19},{19,3},{4,20},{20... | collective-permute-start | bytes 1966088 | tf_op jit(solution)/shard_map/ppermute | solution.py:27
  31.8 7.6 %collective-permute-start.10 = (f32[64,704]{1,0:T(8,128)S(1)}, f32[64,704]{1,0:T(8,128)S(1)}, u32[]{:S(2)}, u32[]{:S(2)}) collective-permute-start(f32[64,704]{1,0:T(8,128)S(1)} %get-tuple-element.66), channel_id=1, source_target_pairs={{0,6},{2,0},{4,2},{6,4},{1,7},{3,1},{5,3},{7,5},{8,14},{10,8},{12,... | collective-permute-start | bytes 540680 | tf_op jit(solution)/shard_map/ppermute | solution.py:27
  32.3 7.1 %collective-permute-start.9 = (f32[64,704]{1,0:T(8,128)S(1)}, f32[64,704]{1,0:T(8,128)S(1)}, u32[]{:S(2)}, u32[]{:S(2)}) collective-permute-start(f32[64,704]{1,0:T(8,128)S(1)} %get-tuple-element.63.refs_7_), channel_id=1, source_target_pairs={{0,2},{2,4},{4,6},{6,0},{1,3},{3,5},{5,7},{7,1},{8,10},{10,12},{12... | collective-permute-start | bytes 540680 | tf_op jit(solution)/shard_map/ppermute | solution.py:27
  39.3 4.9 %collective-permute-start.8 = (f32[192,2816]{1,0:T(8,128)S(1)}, f32[192,2816]{1,0:T(8,128)S(1)}, u32[]{:S(2)}, u32[]{:S(2)}) collective-permute-start(f32[192,2816]{1,0:T(8,128)S(1)} %get-tuple-element.65), channel_id=1, source_target_pairs={{0,8},{8,0},{1,9},{9,1},{2,10},{10,2},{3,11},{11,3},{4,12},{12,4},... | collective-permute-start | bytes 6488072 | tf_op jit(solution)/shard_map/ppermute | solution.py:27
  41.3 2.9 %collective-permute-start.11 = (f32[64,1536]{1,0:T(8,128)S(1)}, f32[64,1536]{1,0:T(8,128)S(1)}, u32[]{:S(2)}, u32[]{:S(2)}) collective-permute-start(f32[64,1536]{1,0:T(8,128)S(1)} %get-tuple-element.68), channel_id=1, source_target_pairs={{0,8},{8,0},{1,9},{9,1},{2,10},{10,2},{3,11},{11,3},{4,12},{12,4},... | collective-permute-start | bytes 1179656 | tf_op jit(solution)/shard_map/ppermute | solution.py:27
  41.9 9.1 %collective-permute-start.12 = (f32[64,1280]{1,0:T(8,128)S(1)}, f32[64,1280]{1,0:T(8,128)S(1)}, u32[]{:S(2)}, u32[]{:S(2)}) collective-permute-start(f32[64,1280]{1,0:T(8,128)S(1)} %get-tuple-element.70), channel_id=1, source_target_pairs={{0,8},{8,0},{1,9},{9,1},{2,10},{10,2},{3,11},{11,3},{4,12},{12,4},... | collective-permute-start | bytes 983048 | tf_op jit(solution)/shard_map/ppermute | solution.py:27
  45.0 13.7 %collective-permute-start.15 = (f32[64,1536]{1,0:T(8,128)S(1)}, f32[64,1536]{1,0:T(8,128)S(1)}, u32[]{:S(2)}, u32[]{:S(2)}) collective-permute-start(f32[64,1536]{1,0:T(8,128)S(1)} %get-tuple-element.71.refs_4_), channel_id=1, source_target_pairs={{0,32},{8,232},{32,64},{40,8},{64,96},{72,40},{96,128},{104,72},{1... | collective-permute-start | bytes 1179656 | tf_op jit(solution)/shard_map/ppermute | solution.py:196
  46.9 12.6 %collective-permute-start.14 = (f32[64,1536]{1,0:T(8,128)S(1)}, f32[64,1536]{1,0:T(8,128)S(1)}, u32[]{:S(2)}, u32[]{:S(2)}) collective-permute-start(f32[64,1536]{1,0:T(8,128)S(1)} %get-tuple-element.72.refs_5_), channel_id=1, source_target_pairs={{0,224},{8,40},{32,0},{40,72},{64,32},{72,104},{96,64},{104,136},{... | collective-permute-start | bytes 1179656 | tf_op jit(solution)/shard_map/ppermute | solution.py:196
  51.0 16.5 %collective-permute-start.18 = (f32[128,1280]{1,0:T(8,128)S(1)}, f32[128,1280]{1,0:T(8,128)S(1)}, u32[]{:S(2)}, u32[]{:S(2)}) collective-permute-start(f32[128,1280]{1,0:T(8,128)S(1)} %shard_map.39.refs_7_), channel_id=1, source_target_pairs={{0,16},{16,0},{1,17},{17,1},{2,18},{18,2},{3,19},{19,3},{4,20},{20... | collective-permute-start | bytes 1966088 | tf_op jit(solution)/shard_map/ppermute | solution.py:27
  58.7 12.9 %collective-permute-start.17 = (f32[64,1536]{1,0:T(8,128)S(1)}, f32[64,1536]{1,0:T(8,128)S(1)}, u32[]{:S(2)}, u32[]{:S(2)}) collective-permute-start(f32[64,1536]{1,0:T(8,128)S(1)} %shard_map.41.refs_2_), channel_id=1, source_target_pairs={{0,32},{8,232},{32,64},{40,8},{64,96},{72,40},{96,128},{104,72},{1... | collective-permute-start | bytes 1179656 | tf_op jit(solution)/shard_map/ppermute | solution.py:196
  59.6 12.1 %collective-permute-start.16 = (f32[64,1536]{1,0:T(8,128)S(1)}, f32[64,1536]{1,0:T(8,128)S(1)}, u32[]{:S(2)}, u32[]{:S(2)}) collective-permute-start(f32[64,1536]{1,0:T(8,128)S(1)} %shard_map.42.refs_9_), channel_id=1, source_target_pairs={{0,224},{8,40},{32,0},{40,72},{64,32},{72,104},{96,64},{104,136},{... | collective-permute-start | bytes 1179656 | tf_op jit(solution)/shard_map/ppermute | solution.py:196
  68.3 7.9 %collective-permute-start.22 = (f32[32,1280]{1,0:T(8,128)S(1)}, f32[32,1280]{1,0:T(8,128)S(1)}, u32[]{:S(2)}, u32[]{:S(2)}) collective-permute-start(f32[32,1280]{1,0:T(8,128)S(1)} %get-tuple-element.78.refs_2_), channel_id=1, source_target_pairs={{0,32},{8,232},{32,64},{40,8},{64,96},{72,40},{96,128},{104,72},{1... | collective-permute-start | bytes 491528 | tf_op jit(solution)/shard_map/ppermute | solution.py:196
  68.4 7.9 %collective-permute-start.21 = (f32[32,1280]{1,0:T(8,128)S(1)}, f32[32,1280]{1,0:T(8,128)S(1)}, u32[]{:S(2)}, u32[]{:S(2)}) collective-permute-start(f32[32,1280]{1,0:T(8,128)S(1)} %get-tuple-element.79.refs_3_), channel_id=1, source_target_pairs={{0,224},{8,40},{32,0},{40,72},{64,32},{72,104},{96,64},{104,136},{... | collective-permute-start | bytes 491528 | tf_op jit(solution)/shard_map/ppermute | solution.py:196
  71.6 12.4 %collective-permute-start.20 = (f32[64,1536]{1,0:T(8,128)S(1)}, f32[64,1536]{1,0:T(8,128)S(1)}, u32[]{:S(2)}, u32[]{:S(2)}) collective-permute-start(f32[64,1536]{1,0:T(8,128)S(1)} %shard_map.44.refs_2_), channel_id=1, source_target_pairs={{0,32},{8,232},{32,64},{40,8},{64,96},{72,40},{96,128},{104,72},{1... | collective-permute-start | bytes 1179656 | tf_op jit(solution)/shard_map/ppermute | solution.py:196
  71.8 12.9 %collective-permute-start.19 = (f32[64,1536]{1,0:T(8,128)S(1)}, f32[64,1536]{1,0:T(8,128)S(1)}, u32[]{:S(2)}, u32[]{:S(2)}) collective-permute-start(f32[64,1536]{1,0:T(8,128)S(1)} %shard_map.45.refs_9_), channel_id=1, source_target_pairs={{0,224},{8,40},{32,0},{40,72},{64,32},{72,104},{96,64},{104,136},{... | collective-permute-start | bytes 1179656 | tf_op jit(solution)/shard_map/ppermute | solution.py:196
  76.2 12.3 %collective-permute-start.24 = (f32[32,1280]{1,0:T(8,128)S(1)}, f32[32,1280]{1,0:T(8,128)S(1)}, u32[]{:S(2)}, u32[]{:S(2)}) collective-permute-start(f32[32,1280]{1,0:T(8,128)S(1)} %shard_map.47.refs_2_), channel_id=1, source_target_pairs={{0,32},{8,232},{32,64},{40,8},{64,96},{72,40},{96,128},{104,72},{1... | collective-permute-start | bytes 491528 | tf_op jit(solution)/shard_map/ppermute | solution.py:196
  76.3 12.3 %collective-permute-start.27 = (f32[32,1280]{1,0:T(8,128)S(1)}, f32[32,1280]{1,0:T(8,128)S(1)}, u32[]{:S(2)}, u32[]{:S(2)}) collective-permute-start(f32[32,1280]{1,0:T(8,128)S(1)} %shard_map.48.refs_2_), channel_id=1, source_target_pairs={{0,224},{8,40},{32,0},{40,72},{64,32},{72,104},{96,64},{104,136},{... | collective-permute-start | bytes 491528 | tf_op jit(solution)/shard_map/ppermute | solution.py:196
  84.0 7.9 %collective-permute-start.26 = (f32[32,1536]{1,0:T(8,128)S(1)}, f32[32,1536]{1,0:T(8,128)S(1)}, u32[]{:S(2)}, u32[]{:S(2)}) collective-permute-start(f32[32,1536]{1,0:T(8,128)S(1)} %shard_map.49.refs_2_), channel_id=1, source_target_pairs={{0,32},{8,232},{32,64},{40,8},{64,96},{72,40},{96,128},{104,72},{1... | collective-permute-start | bytes 589832 | tf_op jit(solution)/shard_map/ppermute | solution.py:196
  84.7 15.4 %collective-permute-start.23 = (f32[32,1536]{1,0:T(8,128)S(1)}, f32[32,1536]{1,0:T(8,128)S(1)}, u32[]{:S(2)}, u32[]{:S(2)}) collective-permute-start(f32[32,1536]{1,0:T(8,128)S(1)} %shard_map.50.refs_2_), channel_id=1, source_target_pairs={{0,224},{8,40},{32,0},{40,72},{64,32},{72,104},{96,64},{104,136},{... | collective-permute-start | bytes 589832 | tf_op jit(solution)/shard_map/ppermute | solution.py:196
  88.5 8.1 %collective-permute-start.25 = (f32[32,1280]{1,0:T(8,128)S(1)}, f32[32,1280]{1,0:T(8,128)S(1)}, u32[]{:S(2)}, u32[]{:S(2)}) collective-permute-start(f32[32,1280]{1,0:T(8,128)S(1)} %shard_map.51.refs_2_), channel_id=1, source_target_pairs={{0,32},{8,232},{32,64},{40,8},{64,96},{72,40},{96,128},{104,72},{1... | collective-permute-start | bytes 491528 | tf_op jit(solution)/shard_map/ppermute | solution.py:196
  88.6 8.1 %collective-permute-start.29 = (f32[32,1280]{1,0:T(8,128)S(1)}, f32[32,1280]{1,0:T(8,128)S(1)}, u32[]{:S(2)}, u32[]{:S(2)}) collective-permute-start(f32[32,1280]{1,0:T(8,128)S(1)} %shard_map.52.refs_3_), channel_id=1, source_target_pairs={{0,224},{8,40},{32,0},{40,72},{64,32},{72,104},{96,64},{104,136},{... | collective-permute-start | bytes 491528 | tf_op jit(solution)/shard_map/ppermute | solution.py:196
  91.9 10.4 %collective-permute-start.31 = (f32[32,1536]{1,0:T(8,128)S(1)}, f32[32,1536]{1,0:T(8,128)S(1)}, u32[]{:S(2)}, u32[]{:S(2)}) collective-permute-start(f32[32,1536]{1,0:T(8,128)S(1)} %shard_map.53.refs_2_), channel_id=1, source_target_pairs={{0,16},{16,0},{1,17},{17,1},{2,18},{18,2},{3,19},{19,3},{4,20},{20... | collective-permute-start | bytes 589832 | tf_op jit(solution)/shard_map/ppermute | solution.py:27
  96.6 5.7 %collective-permute-start.28 = (f32[16,1280]{1,0:T(8,128)S(1)}, f32[16,1280]{1,0:T(8,128)S(1)}, u32[]{:S(2)}, u32[]{:S(2)}) collective-permute-start(f32[16,1280]{1,0:T(8,128)S(1)} %shard_map.54.refs_2_), channel_id=1, source_target_pairs={{0,32},{8,232},{32,64},{40,8},{64,96},{72,40},{96,128},{104,72},{1... | collective-permute-start | bytes 245768 | tf_op jit(solution)/shard_map/ppermute | solution.py:196
  96.7 5.3 %collective-permute-start.30 = (f32[16,1280]{1,0:T(8,128)S(1)}, f32[16,1280]{1,0:T(8,128)S(1)}, u32[]{:S(2)}, u32[]{:S(2)}) collective-permute-start(f32[16,1280]{1,0:T(8,128)S(1)} %shard_map.55.refs_0_), channel_id=1, source_target_pairs={{0,224},{8,40},{32,0},{40,72},{64,32},{72,104},{96,64},{104,136},{... | collective-permute-start | bytes 245768 | tf_op jit(solution)/shard_map/ppermute | solution.py:196
